TPU v7x, 512 devices: a whole 4x4x16 slice. The times are simulated.
512 devices in a mesh: ctx: 32 (over z, y_hi), heads: 16 (over y_lo, x, core).
Axes of the slice: x: 4, y: 4 (y_hi: 2, y_lo: 2; y = y_hi * 2 + y_lo), z: 16, core: 2. Of those that a mesh axis runs over, the one named last changes fastest.
Arguments:
- queries: bfloat16 [8192, 4096], P('ctx', 'heads'), may hold values from -15 to 15
- prefix_keys: bfloat16 [7680, 2048], P('ctx', 'heads'), may hold values from -6 to 6
- prefix_values: bfloat16 [7680, 2048], P('ctx', 'heads'), may hold values from -6 to 6
- suffix_keys: bfloat16 [8192, 2048], P('ctx', 'heads'), may hold values from -10 to 10
- suffix_values: bfloat16 [8192, 2048], P('ctx', 'heads'), may hold values from -6 to 6
- out_weight: bfloat16 [4096, 4608], P('heads'), may hold values from -0.09375 to 0.09375
- lengths: int32 [16], replicated, may hold values from 128 to 512, as said below
- caps: float32 [16], replicated, may hold values from 8 to 50
Outputs:
- attended: float32 [8192, 4608], P(('ctx', 'heads'))
Inputs may be any that keep to these rules, and one draw needn't show every extreme that they name: `lengths`: in every draw at least one request fills all 512 slots.
All inputs are finite; a program needn't handle non-finite values.
Results may differ from a plain program's by a relative error of at most 0.02.
Values may be sent and summed in bfloat16 or wider, within the bound.
No kernel may reach another device: no remote copies, remote signals or barrier semaphores. Data moves between devices by JAX's collectives and lax.ppermute only.
A program may use at most 64 MiB of HBM per device.

v0:
```python
import jax
import jax.numpy as jnp
from jax import lax
from jax.sharding import PartitionSpec as P

GROUP = 2
SUF = 512


score_scale = 1.0 / 12.0


def shifted(value, axis, by):
    size = lax.axis_size(axis)
    return lax.ppermute(value, axis, [(i, (i + by) % size) for i in range(size)])


def attend(query_block, anchor, key_set, key_anchor, lengths, caps):
    query_count = query_block.shape[0]
    suffix_count = query_count // GROUP
    document_count = key_set.shape[1] - suffix_count
    query_index = anchor * suffix_count + jnp.arange(query_count, dtype=jnp.int32) // GROUP
    query_request = query_index // SUF
    query_place = query_index % SUF
    request_ids = jnp.arange(caps.shape[0], dtype=jnp.int32)
    request_match = query_request[:, None] == request_ids[None, :]
    cap_row = jnp.sum(jnp.where(request_match, caps[None, :], 0.0), axis=1)
    length_row = jnp.sum(jnp.where(request_match, lengths[None, :], 0), axis=1)
    key_index = key_anchor * suffix_count + jnp.arange(suffix_count, dtype=jnp.int32)
    key_request = key_index // SUF
    key_place = key_index % SUF
    visible_new = (
        (query_request[:, None] == key_request[None, :])
        & (key_place[None, :] <= query_place[:, None])
        & (key_place[None, :] < length_row[:, None])
    )
    visible = jnp.concatenate(
        [jnp.ones((query_count, document_count), dtype=bool), visible_new], axis=1
    )
    raw_scores = jnp.dot(query_block, key_set[0].T, preferred_element_type=jnp.float32)
    capped = cap_row[:, None] * jnp.tanh(raw_scores * score_scale / cap_row[:, None])
    weights = jnp.where(visible, jnp.exp(capped), 0.0)
    summed = jnp.dot(weights.astype(jnp.bfloat16), key_set[1], preferred_element_type=jnp.float32)
    return (summed, jnp.sum(weights, axis=1))


def local(
    queries, prefix_keys, prefix_values, suffix_keys, suffix_values, out_weight, lengths, caps
):
    query_rows = queries.reshape(queries.shape[0] * GROUP, -1)
    key_set = jnp.stack(
        [
            jnp.concatenate([prefix_keys, suffix_keys], axis=0),
            jnp.concatenate([prefix_values, suffix_values], axis=0),
        ]
    )
    own_index = lax.axis_index("ctx")
    cycle_size = lax.axis_size("ctx")
    first_sum, first_total = attend(query_rows, own_index, key_set, own_index, lengths, caps)

    def key_turn(turn, carry):
        keys_now, summed, totals = carry
        keys_now = shifted(keys_now, "ctx", 1)
        extra_sum, extra_total = attend(
            query_rows, own_index, keys_now, (own_index - turn) % cycle_size, lengths, caps
        )
        return (keys_now, summed + extra_sum, totals + extra_total)

    unused, summed, totals = lax.fori_loop(
        1, cycle_size, key_turn, (key_set, first_sum, first_total)
    )
    mixed = (summed / totals[:, None]).astype(jnp.bfloat16)
    flat_mixed = mixed.reshape(mixed.shape[0] // GROUP, -1)
    return lax.psum_scatter(
        jnp.dot(flat_mixed, out_weight, preferred_element_type=jnp.float32).astype(jnp.bfloat16),
        "heads",
        scatter_dimension=0,
        tiled=True,
    ).astype(jnp.float32)


def solution(mesh):
    return jax.shard_map(
        local,
        mesh=mesh,
        in_specs=(
            P("ctx", "heads"),
            P("ctx", "heads"),
            P("ctx", "heads"),
            P("ctx", "heads"),
            P("ctx", "heads"),
            P("heads", None),
            P(),
            P(),
        ),
        out_specs=P(("ctx", "heads"), None),
        check_vma=False,
    )
```

profile of v0, /device:TPU:1, one launch (start us, length us, event | category | flops | bytes accessed | tf_op | source)
XLA Modules:
  0.0 507.5 jit_solution(11814750481859023191)
XLA Ops:
  13.7 386.8 %while.20 = (s32[]{:T(128)}, bf16[2,496,128]{2,1,0:T(8,128)(2,1)S(1)}, f32[512,128]{1,0:T(8,128)S(1)}, f32[512]{0:T(512)S(1)}, s32[]{:T(128)}, /*index=5*/s32[]{...) while((s32[]{:T(128)}, ...), condition=%wide.region_7.8_spmd, body=%wide.region_3.7_spmd.sunk | while | flops 132335632 | bytes 3744186 | solution.py:69
  19.8 14.3 %collective-permute-done = bf16[2,496,128]{2,1,0:T(8,128)(2,1)S(1)} collective-permute-done((bf16[2,496,128]{2,1,0:T(8,128)(2,1)S(1)}, bf16[2,496,128]{2,1,0:T(8,128)(2,1)S(1)}, u32[]{:S(2)}, u32[]{:S(2)}) %collective-permute-start) | collective-permute-done | bytes 253984 | tf_op jit(solution)/shard_map/while/body/eval_jaxpr/ppermute | solution.py:15
  37.4 9.5 %collective-permute-done = bf16[2,496,128]{2,1,0:T(8,128)(2,1)S(1)} collective-permute-done((bf16[2,496,128]{2,1,0:T(8,128)(2,1)S(1)}, bf16[2,496,128]{2,1,0:T(8,128)(2,1)S(1)}, u32[]{:S(2)}, u32[]{:S(2)}) %collective-permute-start) | collective-permute-done | bytes 253984 | tf_op jit(solution)/shard_map/while/body/eval_jaxpr/ppermute | solution.py:15
  50.2 8.6 %collective-permute-done = bf16[2,496,128]{2,1,0:T(8,128)(2,1)S(1)} collective-permute-done((bf16[2,496,128]{2,1,0:T(8,128)(2,1)S(1)}, bf16[2,496,128]{2,1,0:T(8,128)(2,1)S(1)}, u32[]{:S(2)}, u32[]{:S(2)}) %collective-permute-start) | collective-permute-done | bytes 253984 | tf_op jit(solution)/shard_map/while/body/eval_jaxpr/ppermute | solution.py:15
  62.1 8.3 %collective-permute-done = bf16[2,496,128]{2,1,0:T(8,128)(2,1)S(1)} collective-permute-done((bf16[2,496,128]{2,1,0:T(8,128)(2,1)S(1)}, bf16[2,496,128]{2,1,0:T(8,128)(2,1)S(1)}, u32[]{:S(2)}, u32[]{:S(2)}) %collective-permute-start) | collective-permute-done | bytes 253984 | tf_op jit(solution)/shard_map/while/body/eval_jaxpr/ppermute | solution.py:15
  73.7 8.3 %collective-permute-done = bf16[2,496,128]{2,1,0:T(8,128)(2,1)S(1)} collective-permute-done((bf16[2,496,128]{2,1,0:T(8,128)(2,1)S(1)}, bf16[2,496,128]{2,1,0:T(8,128)(2,1)S(1)}, u32[]{:S(2)}, u32[]{:S(2)}) %collective-permute-start) | collective-permute-done | bytes 253984 | tf_op jit(solution)/shard_map/while/body/eval_jaxpr/ppermute | solution.py:15
  85.2 8.3 %collective-permute-done = bf16[2,496,128]{2,1,0:T(8,128)(2,1)S(1)} collective-permute-done((bf16[2,496,128]{2,1,0:T(8,128)(2,1)S(1)}, bf16[2,496,128]{2,1,0:T(8,128)(2,1)S(1)}, u32[]{:S(2)}, u32[]{:S(2)}) %collective-permute-start) | collective-permute-done | bytes 253984 | tf_op jit(solution)/shard_map/while/body/eval_jaxpr/ppermute | solution.py:15
  96.8 8.3 %collective-permute-done = bf16[2,496,128]{2,1,0:T(8,128)(2,1)S(1)} collective-permute-done((bf16[2,496,128]{2,1,0:T(8,128)(2,1)S(1)}, bf16[2,496,128]{2,1,0:T(8,128)(2,1)S(1)}, u32[]{:S(2)}, u32[]{:S(2)}) %collective-permute-start) | collective-permute-done | bytes 253984 | tf_op jit(solution)/shard_map/while/body/eval_jaxpr/ppermute | solution.py:15
  119.9 8.3 %collective-permute-done = bf16[2,496,128]{2,1,0:T(8,128)(2,1)S(1)} collective-permute-done((bf16[2,496,128]{2,1,0:T(8,128)(2,1)S(1)}, bf16[2,496,128]{2,1,0:T(8,128)(2,1)S(1)}, u32[]{:S(2)}, u32[]{:S(2)}) %collective-permute-start) | collective-permute-done | bytes 253984 | tf_op jit(solution)/shard_map/while/body/eval_jaxpr/ppermute | solution.py:15
  131.5 8.7 %collective-permute-done = bf16[2,496,128]{2,1,0:T(8,128)(2,1)S(1)} collective-permute-done((bf16[2,496,128]{2,1,0:T(8,128)(2,1)S(1)}, bf16[2,496,128]{2,1,0:T(8,128)(2,1)S(1)}, u32[]{:S(2)}, u32[]{:S(2)}) %collective-permute-start) | collective-permute-done | bytes 253984 | tf_op jit(solution)/shard_map/while/body/eval_jaxpr/ppermute | solution.py:15
  143.4 9.8 %collective-permute-done = bf16[2,496,128]{2,1,0:T(8,128)(2,1)S(1)} collective-permute-done((bf16[2,496,128]{2,1,0:T(8,128)(2,1)S(1)}, bf16[2,496,128]{2,1,0:T(8,128)(2,1)S(1)}, u32[]{:S(2)}, u32[]{:S(2)}) %collective-permute-start) | collective-permute-done | bytes 253984 | tf_op jit(solution)/shard_map/while/body/eval_jaxpr/ppermute | solution.py:15
  156.5 11.1 %collective-permute-done = bf16[2,496,128]{2,1,0:T(8,128)(2,1)S(1)} collective-permute-done((bf16[2,496,128]{2,1,0:T(8,128)(2,1)S(1)}, bf16[2,496,128]{2,1,0:T(8,128)(2,1)S(1)}, u32[]{:S(2)}, u32[]{:S(2)}) %collective-permute-start) | collective-permute-done | bytes 253984 | tf_op jit(solution)/shard_map/while/body/eval_jaxpr/ppermute | solution.py:15
  170.9 10.5 %collective-permute-done = bf16[2,496,128]{2,1,0:T(8,128)(2,1)S(1)} collective-permute-done((bf16[2,496,128]{2,1,0:T(8,128)(2,1)S(1)}, bf16[2,496,128]{2,1,0:T(8,128)(2,1)S(1)}, u32[]{:S(2)}, u32[]{:S(2)}) %collective-permute-start) | collective-permute-done | bytes 253984 | tf_op jit(solution)/shard_map/while/body/eval_jaxpr/ppermute | solution.py:15
  184.6 9.5 %collective-permute-done = bf16[2,496,128]{2,1,0:T(8,128)(2,1)S(1)} collective-permute-done((bf16[2,496,128]{2,1,0:T(8,128)(2,1)S(1)}, bf16[2,496,128]{2,1,0:T(8,128)(2,1)S(1)}, u32[]{:S(2)}, u32[]{:S(2)}) %collective-permute-start) | collective-permute-done | bytes 253984 | tf_op jit(solution)/shard_map/while/body/eval_jaxpr/ppermute | solution.py:15
  197.5 8.6 %collective-permute-done = bf16[2,496,128]{2,1,0:T(8,128)(2,1)S(1)} collective-permute-done((bf16[2,496,128]{2,1,0:T(8,128)(2,1)S(1)}, bf16[2,496,128]{2,1,0:T(8,128)(2,1)S(1)}, u32[]{:S(2)}, u32[]{:S(2)}) %collective-permute-start) | collective-permute-done | bytes 253984 | tf_op jit(solution)/shard_map/while/body/eval_jaxpr/ppermute | solution.py:15
  209.4 8.3 %collective-permute-done = bf16[2,496,128]{2,1,0:T(8,128)(2,1)S(1)} collective-permute-done((bf16[2,496,128]{2,1,0:T(8,128)(2,1)S(1)}, bf16[2,496,128]{2,1,0:T(8,128)(2,1)S(1)}, u32[]{:S(2)}, u32[]{:S(2)}) %collective-permute-start) | collective-permute-done | bytes 253984 | tf_op jit(solution)/shard_map/while/body/eval_jaxpr/ppermute | solution.py:15
  220.9 8.3 %collective-permute-done = bf16[2,496,128]{2,1,0:T(8,128)(2,1)S(1)} collective-permute-done((bf16[2,496,128]{2,1,0:T(8,128)(2,1)S(1)}, bf16[2,496,128]{2,1,0:T(8,128)(2,1)S(1)}, u32[]{:S(2)}, u32[]{:S(2)}) %collective-permute-start) | collective-permute-done | bytes 253984 | tf_op jit(solution)/shard_map/while/body/eval_jaxpr/ppermute | solution.py:15
  232.5 8.3 %collective-permute-done = bf16[2,496,128]{2,1,0:T(8,128)(2,1)S(1)} collective-permute-done((bf16[2,496,128]{2,1,0:T(8,128)(2,1)S(1)}, bf16[2,496,128]{2,1,0:T(8,128)(2,1)S(1)}, u32[]{:S(2)}, u32[]{:S(2)}) %collective-permute-start) | collective-permute-done | bytes 253984 | tf_op jit(solution)/shard_map/while/body/eval_jaxpr/ppermute | solution.py:15
  244.0 8.3 %collective-permute-done = bf16[2,496,128]{2,1,0:T(8,128)(2,1)S(1)} collective-permute-done((bf16[2,496,128]{2,1,0:T(8,128)(2,1)S(1)}, bf16[2,496,128]{2,1,0:T(8,128)(2,1)S(1)}, u32[]{:S(2)}, u32[]{:S(2)}) %collective-permute-start) | collective-permute-done | bytes 253984 | tf_op jit(solution)/shard_map/while/body/eval_jaxpr/ppermute | solution.py:15
  255.6 8.3 %collective-permute-done = bf16[2,496,128]{2,1,0:T(8,128)(2,1)S(1)} collective-permute-done((bf16[2,496,128]{2,1,0:T(8,128)(2,1)S(1)}, bf16[2,496,128]{2,1,0:T(8,128)(2,1)S(1)}, u32[]{:S(2)}, u32[]{:S(2)}) %collective-permute-start) | collective-permute-done | bytes 253984 | tf_op jit(solution)/shard_map/while/body/eval_jaxpr/ppermute | solution.py:15
  267.2 8.3 %collective-permute-done = bf16[2,496,128]{2,1,0:T(8,128)(2,1)S(1)} collective-permute-done((bf16[2,496,128]{2,1,0:T(8,128)(2,1)S(1)}, bf16[2,496,128]{2,1,0:T(8,128)(2,1)S(1)}, u32[]{:S(2)}, u32[]{:S(2)}) %collective-permute-start) | collective-permute-done | bytes 253984 | tf_op jit(solution)/shard_map/while/body/eval_jaxpr/ppermute | solution.py:15
  278.7 8.7 %collective-permute-done = bf16[2,496,128]{2,1,0:T(8,128)(2,1)S(1)} collective-permute-done((bf16[2,496,128]{2,1,0:T(8,128)(2,1)S(1)}, bf16[2,496,128]{2,1,0:T(8,128)(2,1)S(1)}, u32[]{:S(2)}, u32[]{:S(2)}) %collective-permute-start) | collective-permute-done | bytes 253984 | tf_op jit(solution)/shard_map/while/body/eval_jaxpr/ppermute | solution.py:15
  290.7 9.8 %collective-permute-done = bf16[2,496,128]{2,1,0:T(8,128)(2,1)S(1)} collective-permute-done((bf16[2,496,128]{2,1,0:T(8,128)(2,1)S(1)}, bf16[2,496,128]{2,1,0:T(8,128)(2,1)S(1)}, u32[]{:S(2)}, u32[]{:S(2)}) %collective-permute-start) | collective-permute-done | bytes 253984 | tf_op jit(solution)/shard_map/while/body/eval_jaxpr/ppermute | solution.py:15
  303.8 11.1 %collective-permute-done = bf16[2,496,128]{2,1,0:T(8,128)(2,1)S(1)} collective-permute-done((bf16[2,496,128]{2,1,0:T(8,128)(2,1)S(1)}, bf16[2,496,128]{2,1,0:T(8,128)(2,1)S(1)}, u32[]{:S(2)}, u32[]{:S(2)}) %collective-permute-start) | collective-permute-done | bytes 253984 | tf_op jit(solution)/shard_map/while/body/eval_jaxpr/ppermute | solution.py:15
  318.2 10.5 %collective-permute-done = bf16[2,496,128]{2,1,0:T(8,128)(2,1)S(1)} collective-permute-done((bf16[2,496,128]{2,1,0:T(8,128)(2,1)S(1)}, bf16[2,496,128]{2,1,0:T(8,128)(2,1)S(1)}, u32[]{:S(2)}, u32[]{:S(2)}) %collective-permute-start) | collective-permute-done | bytes 253984 | tf_op jit(solution)/shard_map/while/body/eval_jaxpr/ppermute | solution.py:15
  331.9 9.5 %collective-permute-done = bf16[2,496,128]{2,1,0:T(8,128)(2,1)S(1)} collective-permute-done((bf16[2,496,128]{2,1,0:T(8,128)(2,1)S(1)}, bf16[2,496,128]{2,1,0:T(8,128)(2,1)S(1)}, u32[]{:S(2)}, u32[]{:S(2)}) %collective-permute-start) | collective-permute-done | bytes 253984 | tf_op jit(solution)/shard_map/while/body/eval_jaxpr/ppermute | solution.py:15
  344.7 8.6 %collective-permute-done = bf16[2,496,128]{2,1,0:T(8,128)(2,1)S(1)} collective-permute-done((bf16[2,496,128]{2,1,0:T(8,128)(2,1)S(1)}, bf16[2,496,128]{2,1,0:T(8,128)(2,1)S(1)}, u32[]{:S(2)}, u32[]{:S(2)}) %collective-permute-start) | collective-permute-done | bytes 253984 | tf_op jit(solution)/shard_map/while/body/eval_jaxpr/ppermute | solution.py:15
  356.6 8.3 %collective-permute-done = bf16[2,496,128]{2,1,0:T(8,128)(2,1)S(1)} collective-permute-done((bf16[2,496,128]{2,1,0:T(8,128)(2,1)S(1)}, bf16[2,496,128]{2,1,0:T(8,128)(2,1)S(1)}, u32[]{:S(2)}, u32[]{:S(2)}) %collective-permute-start) | collective-permute-done | bytes 253984 | tf_op jit(solution)/shard_map/while/body/eval_jaxpr/ppermute | solution.py:15
  368.2 8.3 %collective-permute-done = bf16[2,496,128]{2,1,0:T(8,128)(2,1)S(1)} collective-permute-done((bf16[2,496,128]{2,1,0:T(8,128)(2,1)S(1)}, bf16[2,496,128]{2,1,0:T(8,128)(2,1)S(1)}, u32[]{:S(2)}, u32[]{:S(2)}) %collective-permute-start) | collective-permute-done | bytes 253984 | tf_op jit(solution)/shard_map/while/body/eval_jaxpr/ppermute | solution.py:15
  379.7 8.3 %collective-permute-done = bf16[2,496,128]{2,1,0:T(8,128)(2,1)S(1)} collective-permute-done((bf16[2,496,128]{2,1,0:T(8,128)(2,1)S(1)}, bf16[2,496,128]{2,1,0:T(8,128)(2,1)S(1)}, u32[]{:S(2)}, u32[]{:S(2)}) %collective-permute-start) | collective-permute-done | bytes 253984 | tf_op jit(solution)/shard_map/while/body/eval_jaxpr/ppermute | solution.py:15
  391.3 8.3 %collective-permute-done = bf16[2,496,128]{2,1,0:T(8,128)(2,1)S(1)} collective-permute-done((bf16[2,496,128]{2,1,0:T(8,128)(2,1)S(1)}, bf16[2,496,128]{2,1,0:T(8,128)(2,1)S(1)}, u32[]{:S(2)}, u32[]{:S(2)}) %collective-permute-start) | collective-permute-done | bytes 253984 | tf_op jit(solution)/shard_map/while/body/eval_jaxpr/ppermute | solution.py:15
  402.9 96.1 %reduce-scatter.2.cloned.1.call-done = bf16[16,4608]{1,0:T(8,128)(2,1)} async-done(((bf16[256,4608]{1,0:T(8,128)(2,1)}), bf16[16,4608]{1,0:T(8,128)(2,1)}) %reduce-scatter.2.cloned.1.call-update) | async-done | bytes 147472 | tf_op jit(solution)/shard_map/reduce_scatter | solution.py:74
  (336 shorter events, 122.8 us)
Async XLA Ops:
  6.5 492.5 %reduce-scatter.2.cloned.1.call-start = ((), (), s32[]{:S(2)}) async-start(), calls=%async_computation.1 | async-start | bytes 2506752 | tf_op jit(solution)/shard_map/reduce_scatter | solution.py:74
  13.7 20.4 %collective-permute-start = (bf16[2,496,128]{2,1,0:T(8,128)(2,1)S(1)}, bf16[2,496,128]{2,1,0:T(8,128)(2,1)S(1)}, u32[]{:S(2)}, u32[]{:S(2)}) collective-permute-start(bf16[2,496,128]{2,1,0:T(8,128)(2,1)S(1)} %get-tuple-element.371), channel_id=1, source_target_pairs={{0,16},{16,32},{32,48},{48,64},{64,80},{80,96},{96,112},{112,128},... | collective-permute-start | bytes 761864 | tf_op jit(solution)/shard_map/while/body/eval_jaxpr/ppermute | solution.py:15
  35.0 11.9 %collective-permute-start = (bf16[2,496,128]{2,1,0:T(8,128)(2,1)S(1)}, bf16[2,496,128]{2,1,0:T(8,128)(2,1)S(1)}, u32[]{:S(2)}, u32[]{:S(2)}) collective-permute-start(bf16[2,496,128]{2,1,0:T(8,128)(2,1)S(1)} %get-tuple-element.371), channel_id=1, source_target_pairs={{0,16},{16,32},{32,48},{48,64},{64,80},{80,96},{96,112},{112,128},... | collective-permute-start | bytes 761864 | tf_op jit(solution)/shard_map/while/body/eval_jaxpr/ppermute | solution.py:15
  47.8 11.0 %collective-permute-start = (bf16[2,496,128]{2,1,0:T(8,128)(2,1)S(1)}, bf16[2,496,128]{2,1,0:T(8,128)(2,1)S(1)}, u32[]{:S(2)}, u32[]{:S(2)}) collective-permute-start(bf16[2,496,128]{2,1,0:T(8,128)(2,1)S(1)} %get-tuple-element.371), channel_id=1, source_target_pairs={{0,16},{16,32},{32,48},{48,64},{64,80},{80,96},{96,112},{112,128},... | collective-permute-start | bytes 761864 | tf_op jit(solution)/shard_map/while/body/eval_jaxpr/ppermute | solution.py:15
  59.7 10.6 %collective-permute-start = (bf16[2,496,128]{2,1,0:T(8,128)(2,1)S(1)}, bf16[2,496,128]{2,1,0:T(8,128)(2,1)S(1)}, u32[]{:S(2)}, u32[]{:S(2)}) collective-permute-start(bf16[2,496,128]{2,1,0:T(8,128)(2,1)S(1)} %get-tuple-element.371), channel_id=1, source_target_pairs={{0,16},{16,32},{32,48},{48,64},{64,80},{80,96},{96,112},{112,128},... | collective-permute-start | bytes 761864 | tf_op jit(solution)/shard_map/while/body/eval_jaxpr/ppermute | solution.py:15
  71.3 10.6 %collective-permute-start = (bf16[2,496,128]{2,1,0:T(8,128)(2,1)S(1)}, bf16[2,496,128]{2,1,0:T(8,128)(2,1)S(1)}, u32[]{:S(2)}, u32[]{:S(2)}) collective-permute-start(bf16[2,496,128]{2,1,0:T(8,128)(2,1)S(1)} %get-tuple-element.371), channel_id=1, source_target_pairs={{0,16},{16,32},{32,48},{48,64},{64,80},{80,96},{96,112},{112,128},... | collective-permute-start | bytes 761864 | tf_op jit(solution)/shard_map/while/body/eval_jaxpr/ppermute | solution.py:15
  82.8 10.6 %collective-permute-start = (bf16[2,496,128]{2,1,0:T(8,128)(2,1)S(1)}, bf16[2,496,128]{2,1,0:T(8,128)(2,1)S(1)}, u32[]{:S(2)}, u32[]{:S(2)}) collective-permute-start(bf16[2,496,128]{2,1,0:T(8,128)(2,1)S(1)} %get-tuple-element.371), channel_id=1, source_target_pairs={{0,16},{16,32},{32,48},{48,64},{64,80},{80,96},{96,112},{112,128},... | collective-permute-start | bytes 761864 | tf_op jit(solution)/shard_map/while/body/eval_jaxpr/ppermute | solution.py:15
  94.4 10.6 %collective-permute-start = (bf16[2,496,128]{2,1,0:T(8,128)(2,1)S(1)}, bf16[2,496,128]{2,1,0:T(8,128)(2,1)S(1)}, u32[]{:S(2)}, u32[]{:S(2)}) collective-permute-start(bf16[2,496,128]{2,1,0:T(8,128)(2,1)S(1)} %get-tuple-element.371), channel_id=1, source_target_pairs={{0,16},{16,32},{32,48},{48,64},{64,80},{80,96},{96,112},{112,128},... | collective-permute-start | bytes 761864 | tf_op jit(solution)/shard_map/while/body/eval_jaxpr/ppermute | solution.py:15
  106.0 10.6 %collective-permute-start = (bf16[2,496,128]{2,1,0:T(8,128)(2,1)S(1)}, bf16[2,496,128]{2,1,0:T(8,128)(2,1)S(1)}, u32[]{:S(2)}, u32[]{:S(2)}) collective-permute-start(bf16[2,496,128]{2,1,0:T(8,128)(2,1)S(1)} %get-tuple-element.371), channel_id=1, source_target_pairs={{0,16},{16,32},{32,48},{48,64},{64,80},{80,96},{96,112},{112,128},... | collective-permute-start | bytes 761864 | tf_op jit(solution)/shard_map/while/body/eval_jaxpr/ppermute | solution.py:15
  117.5 10.6 %collective-permute-start = (bf16[2,496,128]{2,1,0:T(8,128)(2,1)S(1)}, bf16[2,496,128]{2,1,0:T(8,128)(2,1)S(1)}, u32[]{:S(2)}, u32[]{:S(2)}) collective-permute-start(bf16[2,496,128]{2,1,0:T(8,128)(2,1)S(1)} %get-tuple-element.371), channel_id=1, source_target_pairs={{0,16},{16,32},{32,48},{48,64},{64,80},{80,96},{96,112},{112,128},... | collective-permute-start | bytes 761864 | tf_op jit(solution)/shard_map/while/body/eval_jaxpr/ppermute | solution.py:15
  129.1 11.1 %collective-permute-start = (bf16[2,496,128]{2,1,0:T(8,128)(2,1)S(1)}, bf16[2,496,128]{2,1,0:T(8,128)(2,1)S(1)}, u32[]{:S(2)}, u32[]{:S(2)}) collective-permute-start(bf16[2,496,128]{2,1,0:T(8,128)(2,1)S(1)} %get-tuple-element.371), channel_id=1, source_target_pairs={{0,16},{16,32},{32,48},{48,64},{64,80},{80,96},{96,112},{112,128},... | collective-permute-start | bytes 761864 | tf_op jit(solution)/shard_map/while/body/eval_jaxpr/ppermute | solution.py:15
  141.1 12.2 %collective-permute-start = (bf16[2,496,128]{2,1,0:T(8,128)(2,1)S(1)}, bf16[2,496,128]{2,1,0:T(8,128)(2,1)S(1)}, u32[]{:S(2)}, u32[]{:S(2)}) collective-permute-start(bf16[2,496,128]{2,1,0:T(8,128)(2,1)S(1)} %get-tuple-element.371), channel_id=1, source_target_pairs={{0,16},{16,32},{32,48},{48,64},{64,80},{80,96},{96,112},{112,128},... | collective-permute-start | bytes 761864 | tf_op jit(solution)/shard_map/while/body/eval_jaxpr/ppermute | solution.py:15
  154.1 13.5 %collective-permute-start = (bf16[2,496,128]{2,1,0:T(8,128)(2,1)S(1)}, bf16[2,496,128]{2,1,0:T(8,128)(2,1)S(1)}, u32[]{:S(2)}, u32[]{:S(2)}) collective-permute-start(bf16[2,496,128]{2,1,0:T(8,128)(2,1)S(1)} %get-tuple-element.371), channel_id=1, source_target_pairs={{0,16},{16,32},{32,48},{48,64},{64,80},{80,96},{96,112},{112,128},... | collective-permute-start | bytes 761864 | tf_op jit(solution)/shard_map/while/body/eval_jaxpr/ppermute | solution.py:15
  168.5 12.8 %collective-permute-start = (bf16[2,496,128]{2,1,0:T(8,128)(2,1)S(1)}, bf16[2,496,128]{2,1,0:T(8,128)(2,1)S(1)}, u32[]{:S(2)}, u32[]{:S(2)}) collective-permute-start(bf16[2,496,128]{2,1,0:T(8,128)(2,1)S(1)} %get-tuple-element.371), channel_id=1, source_target_pairs={{0,16},{16,32},{32,48},{48,64},{64,80},{80,96},{96,112},{112,128},... | collective-permute-start | bytes 761864 | tf_op jit(solution)/shard_map/while/body/eval_jaxpr/ppermute | solution.py:15
  182.3 11.9 %collective-permute-start = (bf16[2,496,128]{2,1,0:T(8,128)(2,1)S(1)}, bf16[2,496,128]{2,1,0:T(8,128)(2,1)S(1)}, u32[]{:S(2)}, u32[]{:S(2)}) collective-permute-start(bf16[2,496,128]{2,1,0:T(8,128)(2,1)S(1)} %get-tuple-element.371), channel_id=1, source_target_pairs={{0,16},{16,32},{32,48},{48,64},{64,80},{80,96},{96,112},{112,128},... | collective-permute-start | bytes 761864 | tf_op jit(solution)/shard_map/while/body/eval_jaxpr/ppermute | solution.py:15
  195.1 11.0 %collective-permute-start = (bf16[2,496,128]{2,1,0:T(8,128)(2,1)S(1)}, bf16[2,496,128]{2,1,0:T(8,128)(2,1)S(1)}, u32[]{:S(2)}, u32[]{:S(2)}) collective-permute-start(bf16[2,496,128]{2,1,0:T(8,128)(2,1)S(1)} %get-tuple-element.371), channel_id=1, source_target_pairs={{0,16},{16,32},{32,48},{48,64},{64,80},{80,96},{96,112},{112,128},... | collective-permute-start | bytes 761864 | tf_op jit(solution)/shard_map/while/body/eval_jaxpr/ppermute | solution.py:15
  207.0 10.6 %collective-permute-start = (bf16[2,496,128]{2,1,0:T(8,128)(2,1)S(1)}, bf16[2,496,128]{2,1,0:T(8,128)(2,1)S(1)}, u32[]{:S(2)}, u32[]{:S(2)}) collective-permute-start(bf16[2,496,128]{2,1,0:T(8,128)(2,1)S(1)} %get-tuple-element.371), channel_id=1, source_target_pairs={{0,16},{16,32},{32,48},{48,64},{64,80},{80,96},{96,112},{112,128},... | collective-permute-start | bytes 761864 | tf_op jit(solution)/shard_map/while/body/eval_jaxpr/ppermute | solution.py:15
  218.5 10.6 %collective-permute-start = (bf16[2,496,128]{2,1,0:T(8,128)(2,1)S(1)}, bf16[2,496,128]{2,1,0:T(8,128)(2,1)S(1)}, u32[]{:S(2)}, u32[]{:S(2)}) collective-permute-start(bf16[2,496,128]{2,1,0:T(8,128)(2,1)S(1)} %get-tuple-element.371), channel_id=1, source_target_pairs={{0,16},{16,32},{32,48},{48,64},{64,80},{80,96},{96,112},{112,128},... | collective-permute-start | bytes 761864 | tf_op jit(solution)/shard_map/while/body/eval_jaxpr/ppermute | solution.py:15
  230.1 10.6 %collective-permute-start = (bf16[2,496,128]{2,1,0:T(8,128)(2,1)S(1)}, bf16[2,496,128]{2,1,0:T(8,128)(2,1)S(1)}, u32[]{:S(2)}, u32[]{:S(2)}) collective-permute-start(bf16[2,496,128]{2,1,0:T(8,128)(2,1)S(1)} %get-tuple-element.371), channel_id=1, source_target_pairs={{0,16},{16,32},{32,48},{48,64},{64,80},{80,96},{96,112},{112,128},... | collective-permute-start | bytes 761864 | tf_op jit(solution)/shard_map/while/body/eval_jaxpr/ppermute | solution.py:15
  241.7 10.6 %collective-permute-start = (bf16[2,496,128]{2,1,0:T(8,128)(2,1)S(1)}, bf16[2,496,128]{2,1,0:T(8,128)(2,1)S(1)}, u32[]{:S(2)}, u32[]{:S(2)}) collective-permute-start(bf16[2,496,128]{2,1,0:T(8,128)(2,1)S(1)} %get-tuple-element.371), channel_id=1, source_target_pairs={{0,16},{16,32},{32,48},{48,64},{64,80},{80,96},{96,112},{112,128},... | collective-permute-start | bytes 761864 | tf_op jit(solution)/shard_map/while/body/eval_jaxpr/ppermute | solution.py:15
  253.2 10.6 %collective-permute-start = (bf16[2,496,128]{2,1,0:T(8,128)(2,1)S(1)}, bf16[2,496,128]{2,1,0:T(8,128)(2,1)S(1)}, u32[]{:S(2)}, u32[]{:S(2)}) collective-permute-start(bf16[2,496,128]{2,1,0:T(8,128)(2,1)S(1)} %get-tuple-element.371), channel_id=1, source_target_pairs={{0,16},{16,32},{32,48},{48,64},{64,80},{80,96},{96,112},{112,128},... | collective-permute-start | bytes 761864 | tf_op jit(solution)/shard_map/while/body/eval_jaxpr/ppermute | solution.py:15
  264.8 10.6 %collective-permute-start = (bf16[2,496,128]{2,1,0:T(8,128)(2,1)S(1)}, bf16[2,496,128]{2,1,0:T(8,128)(2,1)S(1)}, u32[]{:S(2)}, u32[]{:S(2)}) collective-permute-start(bf16[2,496,128]{2,1,0:T(8,128)(2,1)S(1)} %get-tuple-element.371), channel_id=1, source_target_pairs={{0,16},{16,32},{32,48},{48,64},{64,80},{80,96},{96,112},{112,128},... | collective-permute-start | bytes 761864 | tf_op jit(solution)/shard_map/while/body/eval_jaxpr/ppermute | solution.py:15
  276.4 11.1 %collective-permute-start = (bf16[2,496,128]{2,1,0:T(8,128)(2,1)S(1)}, bf16[2,496,128]{2,1,0:T(8,128)(2,1)S(1)}, u32[]{:S(2)}, u32[]{:S(2)}) collective-permute-start(bf16[2,496,128]{2,1,0:T(8,128)(2,1)S(1)} %get-tuple-element.371), channel_id=1, source_target_pairs={{0,16},{16,32},{32,48},{48,64},{64,80},{80,96},{96,112},{112,128},... | collective-permute-start | bytes 761864 | tf_op jit(solution)/shard_map/while/body/eval_jaxpr/ppermute | solution.py:15
  288.3 12.2 %collective-permute-start = (bf16[2,496,128]{2,1,0:T(8,128)(2,1)S(1)}, bf16[2,496,128]{2,1,0:T(8,128)(2,1)S(1)}, u32[]{:S(2)}, u32[]{:S(2)}) collective-permute-start(bf16[2,496,128]{2,1,0:T(8,128)(2,1)S(1)} %get-tuple-element.371), channel_id=1, source_target_pairs={{0,16},{16,32},{32,48},{48,64},{64,80},{80,96},{96,112},{112,128},... | collective-permute-start | bytes 761864 | tf_op jit(solution)/shard_map/while/body/eval_jaxpr/ppermute | solution.py:15
  301.4 13.5 %collective-permute-start = (bf16[2,496,128]{2,1,0:T(8,128)(2,1)S(1)}, bf16[2,496,128]{2,1,0:T(8,128)(2,1)S(1)}, u32[]{:S(2)}, u32[]{:S(2)}) collective-permute-start(bf16[2,496,128]{2,1,0:T(8,128)(2,1)S(1)} %get-tuple-element.371), channel_id=1, source_target_pairs={{0,16},{16,32},{32,48},{48,64},{64,80},{80,96},{96,112},{112,128},... | collective-permute-start | bytes 761864 | tf_op jit(solution)/shard_map/while/body/eval_jaxpr/ppermute | solution.py:15
  315.8 12.8 %collective-permute-start = (bf16[2,496,128]{2,1,0:T(8,128)(2,1)S(1)}, bf16[2,496,128]{2,1,0:T(8,128)(2,1)S(1)}, u32[]{:S(2)}, u32[]{:S(2)}) collective-permute-start(bf16[2,496,128]{2,1,0:T(8,128)(2,1)S(1)} %get-tuple-element.371), channel_id=1, source_target_pairs={{0,16},{16,32},{32,48},{48,64},{64,80},{80,96},{96,112},{112,128},... | collective-permute-start | bytes 761864 | tf_op jit(solution)/shard_map/while/body/eval_jaxpr/ppermute | solution.py:15
  329.5 11.9 %collective-permute-start = (bf16[2,496,128]{2,1,0:T(8,128)(2,1)S(1)}, bf16[2,496,128]{2,1,0:T(8,128)(2,1)S(1)}, u32[]{:S(2)}, u32[]{:S(2)}) collective-permute-start(bf16[2,496,128]{2,1,0:T(8,128)(2,1)S(1)} %get-tuple-element.371), channel_id=1, source_target_pairs={{0,16},{16,32},{32,48},{48,64},{64,80},{80,96},{96,112},{112,128},... | collective-permute-start | bytes 761864 | tf_op jit(solution)/shard_map/while/body/eval_jaxpr/ppermute | solution.py:15
  342.3 11.0 %collective-permute-start = (bf16[2,496,128]{2,1,0:T(8,128)(2,1)S(1)}, bf16[2,496,128]{2,1,0:T(8,128)(2,1)S(1)}, u32[]{:S(2)}, u32[]{:S(2)}) collective-permute-start(bf16[2,496,128]{2,1,0:T(8,128)(2,1)S(1)} %get-tuple-element.371), channel_id=1, source_target_pairs={{0,16},{16,32},{32,48},{48,64},{64,80},{80,96},{96,112},{112,128},... | collective-permute-start | bytes 761864 | tf_op jit(solution)/shard_map/while/body/eval_jaxpr/ppermute | solution.py:15
  354.2 10.6 %collective-permute-start = (bf16[2,496,128]{2,1,0:T(8,128)(2,1)S(1)}, bf16[2,496,128]{2,1,0:T(8,128)(2,1)S(1)}, u32[]{:S(2)}, u32[]{:S(2)}) collective-permute-start(bf16[2,496,128]{2,1,0:T(8,128)(2,1)S(1)} %get-tuple-element.371), channel_id=1, source_target_pairs={{0,16},{16,32},{32,48},{48,64},{64,80},{80,96},{96,112},{112,128},... | collective-permute-start | bytes 761864 | tf_op jit(solution)/shard_map/while/body/eval_jaxpr/ppermute | solution.py:15
  365.8 10.6 %collective-permute-start = (bf16[2,496,128]{2,1,0:T(8,128)(2,1)S(1)}, bf16[2,496,128]{2,1,0:T(8,128)(2,1)S(1)}, u32[]{:S(2)}, u32[]{:S(2)}) collective-permute-start(bf16[2,496,128]{2,1,0:T(8,128)(2,1)S(1)} %get-tuple-element.371), channel_id=1, source_target_pairs={{0,16},{16,32},{32,48},{48,64},{64,80},{80,96},{96,112},{112,128},... | collective-permute-start | bytes 761864 | tf_op jit(solution)/shard_map/while/body/eval_jaxpr/ppermute | solution.py:15
  377.4 10.6 %collective-permute-start = (bf16[2,496,128]{2,1,0:T(8,128)(2,1)S(1)}, bf16[2,496,128]{2,1,0:T(8,128)(2,1)S(1)}, u32[]{:S(2)}, u32[]{:S(2)}) collective-permute-start(bf16[2,496,128]{2,1,0:T(8,128)(2,1)S(1)} %get-tuple-element.371), channel_id=1, source_target_pairs={{0,16},{16,32},{32,48},{48,64},{64,80},{80,96},{96,112},{112,128},... | collective-permute-start | bytes 761864 | tf_op jit(solution)/shard_map/while/body/eval_jaxpr/ppermute | solution.py:15
  388.9 10.6 %collective-permute-start = (bf16[2,496,128]{2,1,0:T(8,128)(2,1)S(1)}, bf16[2,496,128]{2,1,0:T(8,128)(2,1)S(1)}, u32[]{:S(2)}, u32[]{:S(2)}) collective-permute-start(bf16[2,496,128]{2,1,0:T(8,128)(2,1)S(1)} %get-tuple-element.371), channel_id=1, source_target_pairs={{0,16},{16,32},{32,48},{48,64},{64,80},{80,96},{96,112},{112,128},... | collective-permute-start | bytes 761864 | tf_op jit(solution)/shard_map/while/body/eval_jaxpr/ppermute | solution.py:15
  (3 other events, 395.9 us)
Sparse Core Ops, SparseCore 0:
  403.0 95.9 reduce-scatter.1
where the time goes:
time: 510 us; the launch traced here: 507 us
  waiting for transfers between devices  377 us (74%)
  starting transfers between devices  63.3 us (12%)
  matrix products  29.7 us (6%)
  other arithmetic  16.6 us (3%)
  between operations  13.5 us (3%)
    ppermute x31, waiting for transfers between devices, shifted(): lax.ppermute(value, axis, [(i, (i + by) % size) for i in range(size)])  281 us
    reduce_scatter x1, waiting for transfers between devices, local(): lax.psum_scatter(jnp.dot(flat_mixed, out_weight, preferred_element_type=j...  96.1 us
    ppermute x31, starting transfers between devices, shifted(): lax.ppermute(value, axis, [(i, (i + by) % size) for i in range(size)])  63.3 us
    dot_general x32, matrix products, attend(): jnp.dot(query_block, key_set[0].T, preferred_element_type=jnp.float32)  15.7 us
    dot_general x32, matrix products, attend(): jnp.dot(weights.astype(jnp.bfloat16), key_set[1], preferred_element_type=...  11.8 us
  transfers between devices with their start and end apart: 32, of which 32 were waited for; matrix products, arithmetic and copies ran while one was open for 2% of the time, Pallas kernels for 0%

commit v1 on v0

v1 whole, which is shorter than its diff:
```python
import functools
import math

import jax
import jax.numpy as jnp
from jax import lax
from jax.experimental import pallas as pl
from jax.experimental.pallas import tpu as pltpu
from jax.sharding import Mesh
from jax.sharding import PartitionSpec as P

HD = 128
GROUP = 2
SCALE = 1.0 / 12.0
LOG2E = math.log2(math.e)

AXES = ("z321", "z0", "yh", "yl", "x", "c")
SIZES = (8, 2, 2, 2, 4, 2)
CTX = ("z321", "z0", "yh")
HEADS = ("yl", "x", "c")
KEY_AXES = ("z321",)
QUERY_AXES = ("z0", "yh")
PEERS = 4
CHUNK = 640
PIECE = 16
META = 16


def attend_kernel(meta, caps, lengths, q_ref, kv_ref, own_ref, out_ref, acc_ref):
    peer = pl.program_id(0)
    head = pl.program_id(1)
    tokens = q_ref.shape[1]
    keys = kv_ref.shape[0]
    z_base, my_z0, my_yh = meta[0], meta[1], meta[2]
    peer_z0 = peer // 2
    peer_yh = lax.rem(peer, 2)
    request = z_base + peer_z0
    cap = jnp.full((1, 1), caps[request], jnp.float32)
    inner = SCALE / cap
    outer = cap * LOG2E
    q = q_ref[0]

    def weigh(k):
        raw = lax.dot_general(
            q, k, (((1,), (1,)), ((), ())), preferred_element_type=jnp.float32
        )
        return jnp.exp2(outer * jnp.tanh(raw * inner))

    def gather(w, v):
        ones = jnp.ones_like(v)
        return jnp.dot(
            w.astype(jnp.bfloat16),
            jnp.concatenate([v, ones], axis=1),
            preferred_element_type=jnp.float32,
        )

    total = None
    for start in range(0, keys, CHUNK):
        w = weigh(kv_ref[start : start + CHUNK, :HD])
        part = gather(w, kv_ref[start : start + CHUNK, HD:])
        total = part if total is None else total + part
    acc_ref[...] = total

    @pl.when((peer_z0 == my_z0) & (peer_yh >= my_yh))
    def _():
        new_keys = own_ref.shape[0]
        w = weigh(own_ref[:, :HD])
        row = peer_yh * tokens + lax.broadcasted_iota(jnp.int32, w.shape, 0)
        col = my_yh * new_keys + lax.broadcasted_iota(jnp.int32, w.shape, 1)
        seen = (col <= row) & (col < lengths[request])
        acc_ref[...] += gather(jnp.where(seen, w, 0.0), own_ref[:, HD:])

    for c in range(2):
        for j in range(tokens // (2 * PIECE)):
            rows = (2 * j + c) * PIECE
            out_ref[c, j * PIECE : (j + 1) * PIECE, :] = acc_ref[
                rows : rows + PIECE, :HD
            ].astype(out_ref.dtype)
        half = jnp.concatenate(
            [
                acc_ref[(2 * j + c) * PIECE : (2 * j + c + 1) * PIECE, HD:]
                for j in range(tokens // (2 * PIECE))
            ],
            axis=0,
        ).T[:META]
        high = half.astype(jnp.bfloat16).astype(jnp.float32)
        index = lax.broadcasted_iota(jnp.int32, half.shape, 0)
        out_ref[c, tokens // 2 :, :] = jnp.where(index == 0, high, half - high).astype(
            out_ref.dtype
        )


def attend(meta, caps, lengths, q, kv, own):
    peers, tokens, _ = q.shape
    keys = kv.shape[0]
    smem = pl.BlockSpec(memory_space=pltpu.SMEM)
    elements = peers * tokens * GROUP * (keys + own.shape[0] // 2)
    return pl.pallas_call(
        attend_kernel,
        out_shape=jax.ShapeDtypeStruct(
            (peers * 2, tokens // 2 + META, GROUP * HD), jnp.bfloat16
        ),
        grid=(peers, GROUP),
        in_specs=[
            smem,
            smem,
            smem,
            pl.BlockSpec((1, tokens, HD), lambda p, h: (p, 0, h)),
            pl.BlockSpec(kv.shape, lambda p, h: (0, 0)),
            pl.BlockSpec(own.shape, lambda p, h: (0, 0)),
        ],
        out_specs=pl.BlockSpec((2, tokens // 2 + META, HD), lambda p, h: (p, 0, h)),
        scratch_shapes=[pltpu.VMEM((tokens, 2 * HD), jnp.float32)],
        compiler_params=pltpu.CompilerParams(
            dimension_semantics=("arbitrary", "arbitrary"),
            vmem_limit_bytes=40 * 1024 * 1024,
        ),
        cost_estimate=pl.CostEstimate(
            flops=elements * HD * 4,
            bytes_accessed=4 * 1024 * 1024,
            transcendentals=elements * 2,
        ),
        name="attend",
    )(meta, caps, lengths, q, kv, own)


def project_kernel(meta, parts_ref, mine_ref, other_ref, out_ref, mixed_ref):
    half = parts_ref.shape[1] - META
    sources = parts_ref.shape[0] // 2

    @pl.when(pl.program_id(0) == 0)
    def _():
        for core in range(2):
            slot = jnp.where(meta[3] == core, 0, 1)
            for head in range(GROUP):
                cols = slice(head * HD, (head + 1) * HD)
                summed = jnp.zeros((half, HD), jnp.float32)
                totals = jnp.zeros((1, HD), jnp.float32)
                for s in range(sources):
                    block = parts_ref.at[2 * s + core]
                    summed += block[:half, cols].astype(jnp.float32)
                    pair = block[half:, cols].astype(jnp.float32)
                    totals += pair[0:1] + pair[1:2]
                column = jnp.broadcast_to(totals, (HD, HD)).T
                mixed_ref[slot, :, cols] = (summed / column).astype(jnp.bfloat16)

    total = jnp.dot(mixed_ref[0], mine_ref[...], preferred_element_type=jnp.float32)
    total += jnp.dot(mixed_ref[1], other_ref[...], preferred_element_type=jnp.float32)
    out_ref[...] = total.astype(out_ref.dtype)


def project(meta, parts, mine, other):
    half = parts.shape[1] - META
    depth, width = mine.shape
    block = 768
    return pl.pallas_call(
        project_kernel,
        out_shape=jax.ShapeDtypeStruct((half, width), jnp.bfloat16),
        grid=(width // block,),
        in_specs=[
            pl.BlockSpec(memory_space=pltpu.SMEM),
            pl.BlockSpec(parts.shape, lambda i: (0, 0, 0)),
            pl.BlockSpec((depth, block), lambda i: (0, i)),
            pl.BlockSpec((depth, block), lambda i: (0, i)),
        ],
        out_specs=pl.BlockSpec((half, block), lambda i: (0, i)),
        scratch_shapes=[pltpu.VMEM((2, half, GROUP * HD), jnp.bfloat16)],
        compiler_params=pltpu.CompilerParams(
            dimension_semantics=("arbitrary",), vmem_limit_bytes=40 * 1024 * 1024
        ),
        cost_estimate=pl.CostEstimate(
            flops=4 * half * depth * width,
            bytes_accessed=8 * 1024 * 1024,
            transcendentals=0,
        ),
        name="project",
    )(meta, parts, mine, other)


def local(
    queries, prefix_keys, prefix_values, suffix_keys, suffix_values, out_weight, lengths, caps
):
    tokens = queries.shape[0]
    meta = jnp.stack(
        [
            lax.axis_index("z321") * 2,
            lax.axis_index("z0"),
            lax.axis_index("yh"),
            lax.axis_index("c"),
        ]
    ).astype(jnp.int32)
    with jax.named_scope("queries_to_peers"):
        q = lax.all_to_all(
            jnp.broadcast_to(queries[None], (PEERS,) + queries.shape), QUERY_AXES, 0, 0, tiled=True
        )
    with jax.named_scope("weight_swap"):
        other_weight = lax.ppermute(out_weight, "c", [(0, 1), (1, 0)])
    with jax.named_scope("document_gather"):
        kv = lax.all_gather(
            jnp.concatenate([prefix_keys, prefix_values], axis=1), KEY_AXES, axis=0, tiled=True
        )
    own = jnp.concatenate([suffix_keys, suffix_values], axis=1)
    parts = attend(meta, caps, lengths, q, kv, own)
    with jax.named_scope("partials_to_owner"):
        parts = lax.all_to_all(parts, ("z0", "yh", "c"), 0, 0, tiled=True)
    partial = project(meta, parts, out_weight, other_weight)
    with jax.named_scope("heads_exchange"):
        pieces = lax.all_to_all(
            partial.reshape(8, PIECE, -1), ("yl", "x"), 0, 0, tiled=True
        )
    return jnp.sum(pieces.astype(jnp.float32), axis=0)


def solution(mesh):
    fine = Mesh(mesh.devices.reshape(SIZES), AXES)
    return jax.shard_map(
        local,
        mesh=fine,
        in_specs=(
            P(CTX, HEADS),
            P(CTX, HEADS),
            P(CTX, HEADS),
            P(CTX, HEADS),
            P(CTX, HEADS),
            P(HEADS, None),
            P(),
            P(),
        ),
        out_specs=P(CTX + HEADS, None),
        check_vma=False,
    )
```

time: 510 us -> 108 us (0.21)
  waiting for transfers between devices: 377 us -> 9.55 us
  blocking collectives: 0 us -> 52.1 us
  starting transfers between devices: 63.3 us -> 23.5 us
  matrix products: 29.7 us -> 0 us
  Pallas kernels: 0 us -> 16.2 us
  other arithmetic: 16.6 us -> 2.71 us
  between operations: 13.5 us -> 0.05 us
    ppermute x31 -> x1, waiting for transfers between devices: 281 us -> 0.01 us  [local(): other_weight = lax.ppermute(out_weight, 'c', [(0, 1), (1, 0)])]
    reduce_scatter x1 -> x0, waiting for transfers between devices: 96.1 us -> none  [local(): lax.psum_scatter(jnp.dot(flat_mixed, out_weight, preferred_element_type=j...]
    ppermute x31 -> x1, starting transfers between devices: 63.3 us -> 5.9 us  [local(): other_weight = lax.ppermute(out_weight, 'c', [(0, 1), (1, 0)])]
    all_gather x0 -> x1, blocking collectives: none -> 32.7 us  [local(): lax.all_gather(jnp.concatenate([prefix_keys, prefix_values], axis=1), KEY...]
    dot_general x65 -> x0, matrix products: 29.7 us -> none  [the longest x32 15.7 us: attend(): jnp.dot(query_block, key_set[0].T, preferred_element_type=jnp.float32)]
    all_to_all x0 -> x1, blocking collectives: none -> 19.4 us  [local(): lax.all_to_all(partial.reshape(8, PIECE, -1), ('yl', 'x'), 0, 0, tiled=True)]
    all_to_all x0 -> x2, starting transfers between devices: none -> 17.6 us  [the longest x1 11.2 us: local(): parts = lax.all_to_all(parts, ('z0', 'yh', 'c'), 0, 0, tiled=True)]
    pallas_call x0 -> x2, Pallas kernels: none -> 16.2 us  [the longest x1 11.7 us: attend(): pl.pallas_call(attend_kernel, out_shape=jax.ShapeDtypeStruct((peers * 2,...]
  transfers between devices with their start and end apart: 32 -> 3, of which waited for: 32 -> 1; matrix products, arithmetic and copies ran while one was open for 2% -> 2% of each run, Pallas kernels for 0% -> 11%
where the time goes in v1:
time: 108 us; the launch traced here: 107 us
  blocking collectives  52.1 us (48%)
  starting transfers between devices  23.5 us (22%)
  Pallas kernels  16.2 us (15%)
  waiting for transfers between devices  9.55 us (9%)
  local copies, waits for them, and re-layouts  2.97 us (3%)
  other arithmetic  2.71 us (3%)
    all_gather x1, blocking collectives, local(): lax.all_gather(jnp.concatenate([prefix_keys, prefix_values], axis=1), KEY...  32.7 us
    all_to_all x1, blocking collectives, local(): lax.all_to_all(partial.reshape(8, PIECE, -1), ('yl', 'x'), 0, 0, tiled=True)  19.4 us
    pallas_call x1, Pallas kernels, attend(): pl.pallas_call(attend_kernel, out_shape=jax.ShapeDtypeStruct((peers * 2,...  11.7 us
    all_to_all x1, starting transfers between devices, local(): parts = lax.all_to_all(parts, ('z0', 'yh', 'c'), 0, 0, tiled=True)  11.2 us
    all_to_all x1, waiting for transfers between devices, local(): parts = lax.all_to_all(parts, ('z0', 'yh', 'c'), 0, 0, tiled=True)  9.55 us
    all_to_all x1, starting transfers between devices, local(): lax.all_to_all(jnp.broadcast_to(queries[None], (PEERS,) + queries.shape),...  6.37 us
    ppermute x1, starting transfers between devices, local(): other_weight = lax.ppermute(out_weight, 'c', [(0, 1), (1, 0)])  5.9 us
    pallas_call x1, Pallas kernels, project(): pl.pallas_call(project_kernel, out_shape=jax.ShapeDtypeStruct((half, widt...  4.54 us
  transfers between devices with their start and end apart: 3, of which 1 were waited for; matrix products, arithmetic and copies ran while one was open for 2% of the time, Pallas kernels for 11%

profile of v1, /device:TPU:1, one launch (start us, length us, event | category | flops | bytes accessed | tf_op | source)
XLA Modules:
  0.0 107.1 jit_solution(5953350172531065795)
XLA Ops:
  0.0 0.0 copy-start.2
  0.0 0.0 copy-start.3
  0.0 1.8 %broadcast_in_dim.2 = bf16[4,256,256]{2,1,0:T(8,128)(2,1)} broadcast(bf16[256,256]{1,0:T(8,128)(2,1)} %param.8), dimensions={1,2} | broadcast | bytes 655360 | tf_op jit(solution)/shard_map/queries_to_peers/broadcast_in_dim | solution.py:194
  1.8 6.4 %all-to-all-start = ((bf16[4,256,256]{2,1,0:T(8,128)(2,1)}), bf16[4,256,256]{2,1,0:T(8,128)(2,1)S(1)}, u32[]{:S(2)}, u32[]{:S(2)}) async-start(bf16[4,256,256]{2,1,0:T(8,128)(2,1)} %broadcast_in_dim.2), calls=%async_computation | async-start | bytes 1048576 | tf_op jit(solution)/shard_map/queries_to_peers/all_to_all | solution.py:193
  8.1 5.9 %collective-permute-start = (bf16[256,4608]{1,0:T(8,128)(2,1)}, bf16[256,4608]{1,0:T(8,128)(2,1)}, u32[]{:S(2)}, u32[]{:S(2)}) collective-permute-start(bf16[256,4608]{1,0:T(8,128)(2,1)} %mine_ref.1), channel_id=1, source_target_pairs={{0,1},{1,0},{2,3},{3,2},{4,5},{5,4},{6,7},{7,6},{8,9},{9,8},{10,11... | collective-permute-start | bytes 7077896 | tf_op jit(solution)/shard_map/weight_swap/ppermute | solution.py:197
  14.0 0.9 pad_maximum_fusion.1
  14.9 0.9 pad_maximum_fusion.own_ref
  15.8 32.7 %all_gather.3.kv_ref = bf16[1920,256]{1,0:T(8,128)(2,1)} all-gather(bf16[240,256]{1,0:T(8,128)(2,1)S(1)} %pad_maximum_fusion.1), channel_id=1, replica_groups=mesh['z321'=8,'z0'=2,'yh'=2,'yl'=2,'x'=4,'c'=2] {'z321'}, dimensions={0}, use_global_device_ids=true | all-gather | bytes 1105920 | tf_op jit(solution)/shard_map/document_gather/all_gather | solution.py:199
  48.5 0.1 pad_add_fusion.meta
  48.6 0.0 all-to-all-done.q_ref
  48.6 0.0 copy-done.2
  48.6 0.0 copy-done.3
  48.6 0.0 copy-start.1
  48.6 1.2 %copy-done.1 = bf16[1920,256]{1,0:T(8,128)(2,1)S(1)} copy-done((bf16[1920,256]{1,0:T(8,128)(2,1)S(1)}, bf16[1920,256]{1,0:T(8,128)(2,1)}, u32[]{:S(2)}) %copy-start.1) | copy-done | bytes 983064
  49.8 0.0 copy-start
  49.8 11.7 %attend.1 = bf16[8,144,256]{2,1,0:T(8,128)(2,1)} custom-call(s32[4]{0:T(128)S(1)} %pad_add_fusion.meta, f32[16]{0:T(128)S(1)} %copy-done.2, s32[16]{0:T(128)S(1)} %copy-done.3, bf16[4,256,256]{2,1,0:T(8,128)(2,1)S(1)} %all-to-all-done.q_ref, bf16[1920,256]{1,0:T(8,128)(2,1)S(1)} %copy-done.1, bf16[256,256]{1,0:T(8,128)(2,1)S(1)} %pad_maximum_fusion.own_ref), custom_call_target="tpu_custom_call" | custom-call | flops 2147483648 | bytes 4194304 | tf_op jit(solution)/shard_map/attend/pallas_call | solution.py:98
  61.5 11.2 %all-to-all-start.1 = ((bf16[8,144,256]{2,1,0:T(8,128)(2,1)}), bf16[8,144,256]{2,1,0:T(8,128)(2,1)S(1)}, u32[]{:S(2)}, u32[]{:S(2)}) async-start(bf16[8,144,256]{2,1,0:T(8,128)(2,1)} %attend.1), calls=%async_computation.1 | async-start | bytes 1179648 | tf_op jit(solution)/shard_map/partials_to_owner/all_to_all | solution.py:205
  72.8 0.0 collective-permute-done.other_ref
  72.8 9.5 %all-to-all-done.1.parts_ref = bf16[8,144,256]{2,1,0:T(8,128)(2,1)S(1)} async-done(((bf16[8,144,256]{2,1,0:T(8,128)(2,1)}), bf16[8,144,256]{2,1,0:T(8,128)(2,1)S(1)}, u32[]{:S(2)}, u32[]{:S(2)}) %all-to-all-start.1) | async-done | bytes 589856 | tf_op jit(solution)/shard_map/partials_to_owner/all_to_all | solution.py:205
  82.3 0.0 copy-done
  82.3 4.5 %project.1 = bf16[128,4608]{1,0:T(8,128)(2,1)S(1)} custom-call(s32[4]{0:T(128)S(1)} %pad_add_fusion.meta, bf16[8,144,256]{2,1,0:T(8,128)(2,1)S(1)} %all-to-all-done.1.parts_ref, bf16[256,4608]{1,0:T(8,128)(2,1)S(1)} %copy-done, bf16[256,4608]{1,0:T(8,128)(2,1)} %collective-permute-done.other_ref), custom_call_target="tpu_custom_call" | custom-call | flops 603979776 | bytes 8388608 | tf_op jit(solution)/shard_map/project/pallas_call | solution.py:156
  86.9 19.4 %all_to_all.15 = bf16[8,16,4608]{2,1,0:T(8,128)(2,1)S(1)} all-to-all(bf16[8,16,4608]{2,1,0:T(8,128)(2,1)S(1)} %bitcast.5), channel_id=1, replica_groups=mesh['z321'=8,'z0'=2,'yh'=2,'yl'=2,'x'=4,'c'=2] {'yl','x'}, dimensions={0} | all-to-all | bytes 2359296 | tf_op jit(solution)/shard_map/heads_exchange/all_to_all | solution.py:208
  106.3 0.9 convert_reduce_fusion
Async XLA Ops:
  0.0 48.6 %copy-start.2 = (f32[16]{0:T(128)S(1)}, f32[16]{0:T(128)}, u32[]{:S(2)}) copy-start(f32[16]{0:T(128)} %caps.1) | copy-start | bytes 196
  0.0 48.6 %copy-start.3 = (s32[16]{0:T(128)S(1)}, s32[16]{0:T(128)}, u32[]{:S(2)}) copy-start(s32[16]{0:T(128)} %lengths.1) | copy-start | bytes 196
  1.8 46.9 %all-to-all-start = ((bf16[4,256,256]{2,1,0:T(8,128)(2,1)}), bf16[4,256,256]{2,1,0:T(8,128)(2,1)S(1)}, u32[]{:S(2)}, u32[]{:S(2)}) async-start(bf16[4,256,256]{2,1,0:T(8,128)(2,1)} %broadcast_in_dim.2), calls=%async_computation | async-start | bytes 1048576 | tf_op jit(solution)/shard_map/queries_to_peers/all_to_all | solution.py:193
  8.1 64.6 %collective-permute-start = (bf16[256,4608]{1,0:T(8,128)(2,1)}, bf16[256,4608]{1,0:T(8,128)(2,1)}, u32[]{:S(2)}, u32[]{:S(2)}) collective-permute-start(bf16[256,4608]{1,0:T(8,128)(2,1)} %mine_ref.1), channel_id=1, source_target_pairs={{0,1},{1,0},{2,3},{3,2},{4,5},{5,4},{6,7},{7,6},{8,9},{9,8},{10,11... | collective-permute-start | bytes 7077896 | tf_op jit(solution)/shard_map/weight_swap/ppermute | solution.py:197
  48.6 1.2 %copy-start.1 = (bf16[1920,256]{1,0:T(8,128)(2,1)S(1)}, bf16[1920,256]{1,0:T(8,128)(2,1)}, u32[]{:S(2)}) copy-start(bf16[1920,256]{1,0:T(8,128)(2,1)} %all_gather.3.kv_ref) | copy-start | bytes 2949124
  49.8 32.5 %copy-start = (bf16[256,4608]{1,0:T(8,128)(2,1)S(1)}, bf16[256,4608]{1,0:T(8,128)(2,1)}, u32[]{:S(2)}) copy-start(bf16[256,4608]{1,0:T(8,128)(2,1)} %mine_ref.1) | copy-start | bytes 7077892
  61.5 20.8 %all-to-all-start.1 = ((bf16[8,144,256]{2,1,0:T(8,128)(2,1)}), bf16[8,144,256]{2,1,0:T(8,128)(2,1)S(1)}, u32[]{:S(2)}, u32[]{:S(2)}) async-start(bf16[8,144,256]{2,1,0:T(8,128)(2,1)} %attend.1), calls=%async_computation.1 | async-start | bytes 1179648 | tf_op jit(solution)/shard_map/partials_to_owner/all_to_all | solution.py:205

commit v2 on v1

v2 whole, which is shorter than its diff:
```python
import math

import jax
import jax.numpy as jnp
from jax import lax
from jax.experimental import pallas as pl
from jax.experimental.pallas import tpu as pltpu
from jax.sharding import Mesh
from jax.sharding import PartitionSpec as P

HD = 128
GROUP = 2
SCALE = 1.0 / 12.0
LOG2E = math.log2(math.e)

AXES = ("z321", "z0", "yh", "yl", "x", "c")
SIZES = (8, 2, 2, 2, 4, 2)
CTX = ("z321", "z0", "yh")
HEADS = ("yl", "x", "c")
KEY_AXES = ("z321",)
QUERY_AXES = ("z0", "yh")
PEERS = 4
PIECE = 16
META = 16
BLOCK = 768


def attend_kernel(
    meta, caps, lengths, q_ref, kv_ref, new_k_ref, new_v_ref, out_ref, acc_ref
):
    peer = pl.program_id(0)
    tokens = q_ref.shape[1]
    new_keys = new_k_ref.shape[0]
    z_base, my_z0, my_yh = meta[0], meta[1], meta[2]
    peer_z0 = peer // 2
    peer_yh = lax.rem(peer, 2)
    request = z_base + peer_z0
    cap = jnp.full((1, 1), caps[request], jnp.float32)
    inner = SCALE / cap
    outer = cap * LOG2E
    slot = peer
    q = jnp.concatenate(
        [q_ref[slot, :, h * HD : (h + 1) * HD].astype(jnp.bfloat16) for h in range(GROUP)], axis=0
    )

    def weigh(k):
        raw = lax.dot_general(
            q, k, (((1,), (1,)), ((), ())), preferred_element_type=jnp.float32
        )
        return jnp.exp2(outer * jnp.tanh(raw * inner))

    def gather(w, v):
        return jnp.dot(
            w.astype(jnp.bfloat16),
            jnp.concatenate([v, jnp.ones_like(v)], axis=1),
            preferred_element_type=jnp.float32,
        )

    acc_ref[...] = gather(weigh(kv_ref[:, :HD]), kv_ref[:, HD:])

    @pl.when((peer_z0 == my_z0) & (peer_yh >= my_yh))
    def _():
        w = weigh(new_k_ref[...])
        place = lax.broadcasted_iota(jnp.int32, w.shape, 0) % tokens
        row = peer_yh * tokens + place
        col = my_yh * new_keys + lax.broadcasted_iota(jnp.int32, w.shape, 1)
        seen = (col <= row) & (col < lengths[request])
        acc_ref[...] += gather(jnp.where(seen, w, 0.0), new_v_ref[...])

    groups = tokens // (2 * PIECE)
    for head in range(GROUP):
        cols = slice(head * HD, (head + 1) * HD)
        for c in range(2):
            rows = [head * tokens + (2 * j + c) * PIECE for j in range(groups)]
            for j in range(groups):
                out_ref[c, j * PIECE : (j + 1) * PIECE, cols] = acc_ref[
                    rows[j] : rows[j] + PIECE, :HD
                ].astype(out_ref.dtype)
            totals = jnp.concatenate(
                [acc_ref[r : r + PIECE, HD:] for r in rows], axis=0
            ).T[:META]
            high = totals.astype(jnp.bfloat16).astype(jnp.float32)
            index = lax.broadcasted_iota(jnp.int32, totals.shape, 0)
            out_ref[c, tokens // 2 :, cols] = jnp.where(
                index == 0, high, totals - high
            ).astype(out_ref.dtype)


def attend(meta, caps, lengths, q, kv, new_k, new_v):
    _, tokens, _ = q.shape
    keys = kv.shape[0]
    smem = pl.BlockSpec(memory_space=pltpu.SMEM)
    elements = PEERS * tokens * GROUP * (keys + new_k.shape[0] // 2)
    return pl.pallas_call(
        attend_kernel,
        out_shape=jax.ShapeDtypeStruct(
            (PEERS * 2, tokens // 2 + META, GROUP * HD), jnp.bfloat16
        ),
        grid=(PEERS,),
        in_specs=[
            smem,
            smem,
            smem,
            pl.BlockSpec(q.shape, lambda p: (0, 0, 0)),
            pl.BlockSpec(kv.shape, lambda p: (0, 0)),
            pl.BlockSpec(new_k.shape, lambda p: (0, 0)),
            pl.BlockSpec(new_v.shape, lambda p: (0, 0)),
        ],
        out_specs=pl.BlockSpec((2, tokens // 2 + META, GROUP * HD), lambda p: (p, 0, 0)),
        scratch_shapes=[pltpu.VMEM((GROUP * tokens, 2 * HD), jnp.float32)],
        compiler_params=pltpu.CompilerParams(
            dimension_semantics=("arbitrary",),
            vmem_limit_bytes=40 * 1024 * 1024,
        ),
        cost_estimate=pl.CostEstimate(
            flops=elements * HD * 4,
            bytes_accessed=4 * 1024 * 1024,
            transcendentals=elements * 2,
        ),
        name="attend",
    )(meta, caps, lengths, q, kv, new_k, new_v)


def project_kernel(meta, parts_ref, mine_ref, other_ref, out_ref):
    half = parts_ref.shape[1] - META
    sources = parts_ref.shape[0] // 2
    own_core = meta[3]

    def mix(core):
        heads = []
        for head in range(GROUP):
            cols = slice(head * HD, (head + 1) * HD)
            summed = jnp.zeros((half, HD), jnp.float32)
            totals = jnp.zeros((1, HD), jnp.float32)
            for s in range(sources):
                summed += parts_ref[2 * s + core, :half, cols].astype(jnp.float32)
                pair = parts_ref[2 * s + core, half:, cols].astype(jnp.float32)
                totals += pair[0:1] + pair[1:2]
            column = jnp.broadcast_to(totals, (HD, HD)).T
            heads.append((summed / column).astype(jnp.bfloat16))
        return jnp.concatenate(heads, axis=1)

    mine = mix(own_core)
    other = mix(1 - own_core)
    width = out_ref.shape[1]
    for start in range(0, width, BLOCK):
        cols = slice(start, start + BLOCK)
        total = jnp.dot(mine, mine_ref[:, cols], preferred_element_type=jnp.float32)
        total += jnp.dot(other, other_ref[:, cols], preferred_element_type=jnp.float32)
        out_ref[:, cols] = total.astype(out_ref.dtype)


def project(meta, parts, mine, other):
    half = parts.shape[1] - META
    depth, width = mine.shape
    vmem = pl.BlockSpec(memory_space=pltpu.VMEM)
    return pl.pallas_call(
        project_kernel,
        out_shape=jax.ShapeDtypeStruct((half, width), jnp.bfloat16),
        in_specs=[pl.BlockSpec(memory_space=pltpu.SMEM), vmem, vmem, vmem],
        out_specs=vmem,
        compiler_params=pltpu.CompilerParams(vmem_limit_bytes=40 * 1024 * 1024),
        cost_estimate=pl.CostEstimate(
            flops=4 * half * depth * width,
            bytes_accessed=8 * 1024 * 1024,
            transcendentals=0,
        ),
        name="project",
    )(meta, parts, mine, other)


def local(
    queries, prefix_keys, prefix_values, suffix_keys, suffix_values, out_weight, lengths, caps
):
    tokens = queries.shape[0]
    meta = jnp.stack(
        [
            lax.axis_index("z321") * 2,
            lax.axis_index("z0"),
            lax.axis_index("yh"),
            lax.axis_index("c"),
        ]
    ).astype(jnp.int32)
    q = lax.all_to_all(jnp.broadcast_to(queries[None], (PEERS,) + queries.shape), QUERY_AXES, 0, 0, tiled=True)
    weights = (out_weight, lax.ppermute(out_weight, "c", [(0, 1), (1, 0)]))
    with jax.named_scope("document_gather"):
        kv = lax.all_gather(
            jnp.concatenate([prefix_keys, prefix_values], axis=1), KEY_AXES, axis=0, tiled=True
        )
    parts = attend(meta, caps, lengths, q, kv, suffix_keys, suffix_values)
    with jax.named_scope("partials_to_owner"):
        parts = lax.all_to_all(parts, ("z0", "yh", "c"), 0, 0, tiled=True)
    partial = project(meta, parts, *weights)
    with jax.named_scope("heads_exchange"):
        pieces = lax.all_to_all(
            partial.reshape(8, PIECE, -1), ("yl", "x"), 0, 0, tiled=True
        )
    return jnp.sum(pieces.astype(jnp.float32), axis=0)


def solution(mesh):
    fine = Mesh(mesh.devices.reshape(SIZES), AXES)
    return jax.shard_map(
        local,
        mesh=fine,
        in_specs=(
            P(CTX, HEADS),
            P(CTX, HEADS),
            P(CTX, HEADS),
            P(CTX, HEADS),
            P(CTX, HEADS),
            P(HEADS, None),
            P(),
            P(),
        ),
        out_specs=P(CTX + HEADS, None),
        check_vma=False,
    )
```

time: 108 us -> 102 us (0.944)
  Pallas kernels: 16.2 us -> 10.8 us
    pallas_call x1, Pallas kernels: 11.7 us -> 8.26 us  [attend(): pl.pallas_call(attend_kernel, out_shape=jax.ShapeDtypeStruct((PEERS * 2,...]
    pallas_call x1, Pallas kernels: 4.54 us -> 2.53 us  [project(): pl.pallas_call(project_kernel, out_shape=jax.ShapeDtypeStruct((half, widt...]
  transfers between devices with their start and end apart: 3 -> 3, of which waited for: 1 -> 1; matrix products, arithmetic and copies ran while one was open for 2% -> 1% of each run, Pallas kernels for 11% -> 8%
where the time goes in v2:
time: 102 us; the launch traced here: 101 us
  blocking collectives  52.1 us (51%)
  starting transfers between devices  23.7 us (23%)
  Pallas kernels  10.8 us (11%)
  waiting for transfers between devices  9.55 us (9%)
  local copies, waits for them, and re-layouts  2.99 us (3%)
  other arithmetic  1.82 us (2%)
    all_gather x1, blocking collectives, local(): lax.all_gather(jnp.concatenate([prefix_keys, prefix_values], axis=1), KEY...  32.6 us
    all_to_all x1, blocking collectives, local(): lax.all_to_all(partial.reshape(8, PIECE, -1), ('yl', 'x'), 0, 0, tiled=True)  19.4 us
    all_to_all x1, starting transfers between devices, local(): parts = lax.all_to_all(parts, ('z0', 'yh', 'c'), 0, 0, tiled=True)  11.5 us
    all_to_all x1, waiting for transfers between devices, local(): parts = lax.all_to_all(parts, ('z0', 'yh', 'c'), 0, 0, tiled=True)  9.55 us
    pallas_call x1, Pallas kernels, attend(): pl.pallas_call(attend_kernel, out_shape=jax.ShapeDtypeStruct((PEERS * 2,...  8.26 us
    all_to_all x1, starting transfers between devices, local(): lax.all_to_all(jnp.broadcast_to(queries[None], (PEERS,) + queries.shape),...  6.37 us
    ppermute x1, starting transfers between devices, local(): weights = (out_weight, lax.ppermute(out_weight, 'c', [(0, 1), (1, 0)]))  5.87 us
    pallas_call x1, Pallas kernels, project(): pl.pallas_call(project_kernel, out_shape=jax.ShapeDtypeStruct((half, widt...  2.53 us
  transfers between devices with their start and end apart: 3, of which 1 were waited for; matrix products, arithmetic and copies ran while one was open for 1% of the time, Pallas kernels for 8%

profile of v2, /device:TPU:1, one launch (start us, length us, event | category | flops | bytes accessed | tf_op | source)
XLA Modules:
  0.0 101.0 jit_solution(12113951825036066270)
XLA Ops:
  0.0 0.0 copy-start.4
  0.0 0.0 copy-start.5
  0.0 0.0 copy-start.3
  0.0 0.0 copy-start.2
  0.0 1.8 %broadcast_in_dim.2 = bf16[4,256,256]{2,1,0:T(8,128)(2,1)} broadcast(bf16[256,256]{1,0:T(8,128)(2,1)} %param.8), dimensions={1,2} | broadcast | bytes 655360 | tf_op jit(solution)/shard_map/broadcast_in_dim | solution.py:184
  1.8 6.4 %all-to-all-start = ((bf16[4,256,256]{2,1,0:T(8,128)(2,1)}), bf16[4,256,256]{2,1,0:T(8,128)(2,1)S(1)}, u32[]{:S(2)}, u32[]{:S(2)}) async-start(bf16[4,256,256]{2,1,0:T(8,128)(2,1)} %broadcast_in_dim.2), calls=%async_computation | async-start | bytes 1048576 | tf_op jit(solution)/shard_map/all_to_all | solution.py:184
  8.2 5.9 %collective-permute-start = (bf16[256,4608]{1,0:T(8,128)(2,1)}, bf16[256,4608]{1,0:T(8,128)(2,1)}, u32[]{:S(2)}, u32[]{:S(2)}) collective-permute-start(bf16[256,4608]{1,0:T(8,128)(2,1)} %mine_ref.1), channel_id=1, source_target_pairs={{0,1},{1,0},{2,3},{3,2},{4,5},{5,4},{6,7},{7,6},{8,9},{9,8},{10,11... | collective-permute-start | bytes 7077896 | tf_op jit(solution)/shard_map/ppermute | solution.py:185
  14.1 0.9 pad_maximum_fusion
  14.9 32.6 %all_gather.3.kv_ref = bf16[1920,256]{1,0:T(8,128)(2,1)} all-gather(bf16[240,256]{1,0:T(8,128)(2,1)S(1)} %pad_maximum_fusion), channel_id=1, replica_groups=mesh['z321'=8,'z0'=2,'yh'=2,'yl'=2,'x'=4,'c'=2] {'z321'}, dimensions={0}, use_global_device_ids=true | all-gather | bytes 1105920 | tf_op jit(solution)/shard_map/document_gather/all_gather | solution.py:187
  47.6 0.1 pad_add_fusion.meta
  47.7 0.0 all-to-all-done.q_ref
  47.7 0.0 copy-done.4
  47.7 0.0 copy-done.5
  47.7 0.0 copy-done.3
  47.7 0.0 copy-done.2
  47.7 0.0 copy-start.1
  47.7 1.2 %copy-done.1 = bf16[1920,256]{1,0:T(8,128)(2,1)S(1)} copy-done((bf16[1920,256]{1,0:T(8,128)(2,1)S(1)}, bf16[1920,256]{1,0:T(8,128)(2,1)}, u32[]{:S(2)}) %copy-start.1) | copy-done | bytes 983064
  48.9 0.0 copy-start
  48.9 8.3 %attend.1 = bf16[8,144,256]{2,1,0:T(8,128)(2,1)} custom-call(s32[4]{0:T(128)S(1)} %pad_add_fusion.meta, f32[16]{0:T(128)S(1)} %copy-done.4, s32[16]{0:T(128)S(1)} %copy-done.5, bf16[4,256,256]{2,1,0:T(8,128)(2,1)S(1)} %all-to-all-done.q_ref, bf16[1920,256]{1,0:T(8,128)(2,1)S(1)} %copy-done.1, bf16[256,128]{1,0:T(8,128)(2,1)S(1)} %copy-done.2, ...), custom_call_target="tpu_custom_call" | custom-call | flops 2147483648 | bytes 4194304 | tf_op jit(solution)/shard_map/attend/pallas_call | solution.py:94
  57.1 11.5 %all-to-all-start.1 = ((bf16[8,144,256]{2,1,0:T(8,128)(2,1)}), bf16[8,144,256]{2,1,0:T(8,128)(2,1)S(1)}, u32[]{:S(2)}, u32[]{:S(2)}) async-start(bf16[8,144,256]{2,1,0:T(8,128)(2,1)} %attend.1), calls=%async_computation.1 | async-start | bytes 1179648 | tf_op jit(solution)/shard_map/partials_to_owner/all_to_all | solution.py:192
  68.6 0.0 collective-permute-done.other_ref
  68.6 9.5 %all-to-all-done.1.parts_ref = bf16[8,144,256]{2,1,0:T(8,128)(2,1)S(1)} async-done(((bf16[8,144,256]{2,1,0:T(8,128)(2,1)}), bf16[8,144,256]{2,1,0:T(8,128)(2,1)S(1)}, u32[]{:S(2)}, u32[]{:S(2)}) %all-to-all-start.1) | async-done | bytes 589856 | tf_op jit(solution)/shard_map/partials_to_owner/all_to_all | solution.py:192
  78.2 0.0 copy-done
  78.2 2.5 %project.1 = bf16[128,4608]{1,0:T(8,128)(2,1)S(1)} custom-call(s32[4]{0:T(128)S(1)} %pad_add_fusion.meta, bf16[8,144,256]{2,1,0:T(8,128)(2,1)S(1)} %all-to-all-done.1.parts_ref, bf16[256,4608]{1,0:T(8,128)(2,1)S(1)} %copy-done, bf16[256,4608]{1,0:T(8,128)(2,1)} %collective-permute-done.other_ref), custom_call_target="tpu_custom_call" | custom-call | flops 603979776 | bytes 8388608 | tf_op jit(solution)/shard_map/project/pallas_call | solution.py:157
  80.7 19.4 %all_to_all.15 = bf16[8,16,4608]{2,1,0:T(8,128)(2,1)S(1)} all-to-all(bf16[8,16,4608]{2,1,0:T(8,128)(2,1)S(1)} %bitcast.5), channel_id=1, replica_groups=mesh['z321'=8,'z0'=2,'yh'=2,'yl'=2,'x'=4,'c'=2] {'yl','x'}, dimensions={0} | all-to-all | bytes 2359296 | tf_op jit(solution)/shard_map/heads_exchange/all_to_all | solution.py:195
  100.1 0.9 convert_reduce_fusion
Async XLA Ops:
  0.0 47.7 %copy-start.4 = (f32[16]{0:T(128)S(1)}, f32[16]{0:T(128)}, u32[]{:S(2)}) copy-start(f32[16]{0:T(128)} %caps.1) | copy-start | bytes 196
  0.0 47.7 %copy-start.5 = (s32[16]{0:T(128)S(1)}, s32[16]{0:T(128)}, u32[]{:S(2)}) copy-start(s32[16]{0:T(128)} %lengths.1) | copy-start | bytes 196
  0.0 47.7 %copy-start.3 = (bf16[256,128]{1,0:T(8,128)(2,1)S(1)}, bf16[256,128]{1,0:T(8,128)(2,1)}, u32[]{:S(2)}) copy-start(bf16[256,128]{1,0:T(8,128)(2,1)} %new_v_ref.1) | copy-start | bytes 196612
  0.0 47.7 %copy-start.2 = (bf16[256,128]{1,0:T(8,128)(2,1)S(1)}, bf16[256,128]{1,0:T(8,128)(2,1)}, u32[]{:S(2)}) copy-start(bf16[256,128]{1,0:T(8,128)(2,1)} %new_k_ref.1) | copy-start | bytes 196612
  1.8 45.9 %all-to-all-start = ((bf16[4,256,256]{2,1,0:T(8,128)(2,1)}), bf16[4,256,256]{2,1,0:T(8,128)(2,1)S(1)}, u32[]{:S(2)}, u32[]{:S(2)}) async-start(bf16[4,256,256]{2,1,0:T(8,128)(2,1)} %broadcast_in_dim.2), calls=%async_computation | async-start | bytes 1048576 | tf_op jit(solution)/shard_map/all_to_all | solution.py:184
  8.2 60.5 %collective-permute-start = (bf16[256,4608]{1,0:T(8,128)(2,1)}, bf16[256,4608]{1,0:T(8,128)(2,1)}, u32[]{:S(2)}, u32[]{:S(2)}) collective-permute-start(bf16[256,4608]{1,0:T(8,128)(2,1)} %mine_ref.1), channel_id=1, source_target_pairs={{0,1},{1,0},{2,3},{3,2},{4,5},{5,4},{6,7},{7,6},{8,9},{9,8},{10,11... | collective-permute-start | bytes 7077896 | tf_op jit(solution)/shard_map/ppermute | solution.py:185
  47.7 1.2 %copy-start.1 = (bf16[1920,256]{1,0:T(8,128)(2,1)S(1)}, bf16[1920,256]{1,0:T(8,128)(2,1)}, u32[]{:S(2)}) copy-start(bf16[1920,256]{1,0:T(8,128)(2,1)} %all_gather.3.kv_ref) | copy-start | bytes 2949124
  48.9 29.3 %copy-start = (bf16[256,4608]{1,0:T(8,128)(2,1)S(1)}, bf16[256,4608]{1,0:T(8,128)(2,1)}, u32[]{:S(2)}) copy-start(bf16[256,4608]{1,0:T(8,128)(2,1)} %mine_ref.1) | copy-start | bytes 7077892
  57.1 21.0 %all-to-all-start.1 = ((bf16[8,144,256]{2,1,0:T(8,128)(2,1)}), bf16[8,144,256]{2,1,0:T(8,128)(2,1)S(1)}, u32[]{:S(2)}, u32[]{:S(2)}) async-start(bf16[8,144,256]{2,1,0:T(8,128)(2,1)} %attend.1), calls=%async_computation.1 | async-start | bytes 1179648 | tf_op jit(solution)/shard_map/partials_to_owner/all_to_all | solution.py:192

commit v3 on v2

--- a/solution.py
+++ b/solution.py
@@ -25,91 +25,119 @@
 BLOCK = 768
 
 
+def prepare_kernel(q_ref, k_ref, v_ref, copies_ref, kv_ref):
+    kv_ref[:, :HD] = k_ref[...]
+    kv_ref[:, HD:] = v_ref[...]
+    for peer in range(PEERS):
+        copies_ref[peer] = q_ref[...]
+
+
+def prepare(q, k, v):
+    vmem = pl.BlockSpec(memory_space=pltpu.VMEM)
+    return pl.pallas_call(
+        prepare_kernel,
+        out_shape=(
+            jax.ShapeDtypeStruct((PEERS,) + q.shape, q.dtype),
+            jax.ShapeDtypeStruct((k.shape[0], 2 * HD), k.dtype),
+        ),
+        in_specs=[vmem] * 3,
+        out_specs=(vmem, vmem),
+        name="prepare",
+    )(q, k, v)
+
+
 def attend_kernel(
     meta, caps, lengths, q_ref, kv_ref, new_k_ref, new_v_ref, out_ref, acc_ref
 ):
-    peer = pl.program_id(0)
-    tokens = q_ref.shape[1]
-    new_keys = new_k_ref.shape[0]
-    z_base, my_z0, my_yh = meta[0], meta[1], meta[2]
-    peer_z0 = peer // 2
-    peer_yh = lax.rem(peer, 2)
-    request = z_base + peer_z0
-    cap = jnp.full((1, 1), caps[request], jnp.float32)
-    inner = SCALE / cap
-    outer = cap * LOG2E
-    slot = peer
-    q = jnp.concatenate(
-        [q_ref[slot, :, h * HD : (h + 1) * HD].astype(jnp.bfloat16) for h in range(GROUP)], axis=0
-    )
-
-    def weigh(k):
-        raw = lax.dot_general(
-            q, k, (((1,), (1,)), ((), ())), preferred_element_type=jnp.float32
+    def serve(peer):
+        tokens = q_ref.shape[1]
+        new_keys = new_k_ref.shape[0]
+        z_base, my_z0, my_yh = meta[0], meta[1], meta[2]
+        peer_z0 = peer // 2
+        peer_yh = lax.rem(peer, 2)
+        request = z_base + peer_z0
+        cap = jnp.full((1, 1), caps[request], jnp.float32)
+        inner = SCALE / cap
+        outer = cap * LOG2E
+        slot = peer
+        q = jnp.concatenate(
+            [q_ref[slot, :, h * HD : (h + 1) * HD].astype(jnp.bfloat16) for h in range(GROUP)], axis=0
         )
-        return jnp.exp2(outer * jnp.tanh(raw * inner))
-
-    def gather(w, v):
-        return jnp.dot(
-            w.astype(jnp.bfloat16),
-            jnp.concatenate([v, jnp.ones_like(v)], axis=1),
-            preferred_element_type=jnp.float32,
-        )
-
-    acc_ref[...] = gather(weigh(kv_ref[:, :HD]), kv_ref[:, HD:])
-
-    @pl.when((peer_z0 == my_z0) & (peer_yh >= my_yh))
-    def _():
-        w = weigh(new_k_ref[...])
-        place = lax.broadcasted_iota(jnp.int32, w.shape, 0) % tokens
-        row = peer_yh * tokens + place
-        col = my_yh * new_keys + lax.broadcasted_iota(jnp.int32, w.shape, 1)
-        seen = (col <= row) & (col < lengths[request])
-        acc_ref[...] += gather(jnp.where(seen, w, 0.0), new_v_ref[...])
-
-    groups = tokens // (2 * PIECE)
-    for head in range(GROUP):
-        cols = slice(head * HD, (head + 1) * HD)
-        for c in range(2):
-            rows = [head * tokens + (2 * j + c) * PIECE for j in range(groups)]
-            for j in range(groups):
-                out_ref[c, j * PIECE : (j + 1) * PIECE, cols] = acc_ref[
-                    rows[j] : rows[j] + PIECE, :HD
-                ].astype(out_ref.dtype)
-            totals = jnp.concatenate(
-                [acc_ref[r : r + PIECE, HD:] for r in rows], axis=0
-            ).T[:META]
-            high = totals.astype(jnp.bfloat16).astype(jnp.float32)
-            index = lax.broadcasted_iota(jnp.int32, totals.shape, 0)
-            out_ref[c, tokens // 2 :, cols] = jnp.where(
-                index == 0, high, totals - high
-            ).astype(out_ref.dtype)
+
+        def weigh(k):
+            raw = lax.dot_general(
+                q, k, (((1,), (1,)), ((), ())), preferred_element_type=jnp.float32
+            )
+            return jnp.exp2(outer * jnp.tanh(raw * inner))
+
+        def gather(w, v):
+            return jnp.dot(
+                w.astype(jnp.bfloat16),
+                jnp.concatenate([v, jnp.ones_like(v)], axis=1),
+                preferred_element_type=jnp.float32,
+            )
+
+        def document():
+            return gather(weigh(kv_ref[:, :HD]), kv_ref[:, HD:])
+
+        def suffix():
+            w = weigh(new_k_ref[...])
+            place = lax.broadcasted_iota(jnp.int32, w.shape, 0) % tokens
+            row = peer_yh * tokens + place
+            col = my_yh * new_keys + lax.broadcasted_iota(jnp.int32, w.shape, 1)
+            seen = (col <= row) & (col < lengths[request])
+            return gather(jnp.where(seen, w, 0.0), new_v_ref[...])
+
+        sees_suffix = (peer_z0 == my_z0) & (peer_yh >= my_yh)
+
+        @pl.when(sees_suffix)
+        def _():
+            acc_ref[...] = suffix() + document()
+
+        @pl.when(jnp.logical_not(sees_suffix))
+        def _():
+            acc_ref[...] = document()
+
+        groups = tokens // (2 * PIECE)
+        for head in range(GROUP):
+            cols = slice(head * HD, (head + 1) * HD)
+            for c in range(2):
+                rows = [head * tokens + (2 * j + c) * PIECE for j in range(groups)]
+                for j in range(groups):
+                    out_ref[2 * peer + c, j * PIECE : (j + 1) * PIECE, cols] = acc_ref[
+                        rows[j] : rows[j] + PIECE, :HD
+                    ].astype(out_ref.dtype)
+                totals = jnp.concatenate(
+                    [acc_ref[r : r + PIECE, HD:] for r in rows], axis=0
+                ).T[:META]
+                high = totals.astype(jnp.bfloat16).astype(jnp.float32)
+                index = lax.broadcasted_iota(jnp.int32, totals.shape, 0)
+                out_ref[2 * peer + c, tokens // 2 :, cols] = jnp.where(
+                    index == 0, high, totals - high
+                ).astype(out_ref.dtype)
+
+    def step(peer, carry):
+        serve(peer)
+        return carry
+
+    lax.fori_loop(0, PEERS, step, 0)
 
 
 def attend(meta, caps, lengths, q, kv, new_k, new_v):
     _, tokens, _ = q.shape
     keys = kv.shape[0]
     smem = pl.BlockSpec(memory_space=pltpu.SMEM)
+    vmem = pl.BlockSpec(memory_space=pltpu.VMEM)
     elements = PEERS * tokens * GROUP * (keys + new_k.shape[0] // 2)
     return pl.pallas_call(
         attend_kernel,
         out_shape=jax.ShapeDtypeStruct(
             (PEERS * 2, tokens // 2 + META, GROUP * HD), jnp.bfloat16
         ),
-        grid=(PEERS,),
-        in_specs=[
-            smem,
-            smem,
-            smem,
-            pl.BlockSpec(q.shape, lambda p: (0, 0, 0)),
-            pl.BlockSpec(kv.shape, lambda p: (0, 0)),
-            pl.BlockSpec(new_k.shape, lambda p: (0, 0)),
-            pl.BlockSpec(new_v.shape, lambda p: (0, 0)),
-        ],
-        out_specs=pl.BlockSpec((2, tokens // 2 + META, GROUP * HD), lambda p: (p, 0, 0)),
+        in_specs=[smem, smem, smem, vmem, vmem, vmem, vmem],
+        out_specs=vmem,
         scratch_shapes=[pltpu.VMEM((GROUP * tokens, 2 * HD), jnp.float32)],
         compiler_params=pltpu.CompilerParams(
-            dimension_semantics=("arbitrary",),
             vmem_limit_bytes=40 * 1024 * 1024,
         ),
         cost_estimate=pl.CostEstimate(
@@ -181,15 +209,17 @@
             lax.axis_index("c"),
         ]
     ).astype(jnp.int32)
-    q = lax.all_to_all(jnp.broadcast_to(queries[None], (PEERS,) + queries.shape), QUERY_AXES, 0, 0, tiled=True)
-    weights = (out_weight, lax.ppermute(out_weight, "c", [(0, 1), (1, 0)]))
+    copies, pair = prepare(queries, prefix_keys, prefix_values)
+    q = lax.all_to_all(copies, QUERY_AXES, 0, 0, tiled=True)
     with jax.named_scope("document_gather"):
         kv = lax.all_gather(
-            jnp.concatenate([prefix_keys, prefix_values], axis=1), KEY_AXES, axis=0, tiled=True
+            pair, KEY_AXES, axis=0, tiled=True
         )
     parts = attend(meta, caps, lengths, q, kv, suffix_keys, suffix_values)
+    late_weight, parts = lax.optimization_barrier((out_weight, parts))
     with jax.named_scope("partials_to_owner"):
         parts = lax.all_to_all(parts, ("z0", "yh", "c"), 0, 0, tiled=True)
+    weights = (out_weight, lax.ppermute(late_weight, "c", [(0, 1), (1, 0)]))
     partial = project(meta, parts, *weights)
     with jax.named_scope("heads_exchange"):
         pieces = lax.all_to_all(

time: 102 us -> 101 us (level)
  blocking collectives: 52.1 us -> 73.1 us
  waiting for transfers between devices: 9.55 us -> 0.01 us
  starting transfers between devices: 23.7 us -> 14.9 us
  local copies, waits for them, and re-layouts: 2.99 us -> 0.02 us
    all_to_all x0 -> x1, blocking collectives: none -> 15.1 us  [local(): parts = lax.all_to_all(parts, ('z0', 'yh', 'c'), 0, 0, tiled=True)]
    all_to_all x2 -> x1, starting transfers between devices: 17.8 us -> 6.37 us  [local(): q = lax.all_to_all(copies, QUERY_AXES, 0, 0, tiled=True)]
    all_to_all x2 -> x1, waiting for transfers between devices: 9.55 us -> 0.01 us  [local(): q = lax.all_to_all(copies, QUERY_AXES, 0, 0, tiled=True)]
    all_gather x1, blocking collectives: 32.6 us -> 38.3 us  [local(): kv = lax.all_gather(pair, KEY_AXES, axis=0, tiled=True)]
    ppermute x1, starting transfers between devices: 5.87 us -> 8.55 us  [local(): weights = (out_weight, lax.ppermute(late_weight, 'c', [(0, 1), (1, 0)]))]
    pallas_call x0 -> x1, Pallas kernels: none -> 1.85 us  [prepare(): pl.pallas_call(prepare_kernel, out_shape=(jax.ShapeDtypeStruct((PEERS,) +...]
    broadcast_in_dim x1 -> x0, local copies, waits for them, and re-layouts: 1.78 us -> none  [local(): jnp.broadcast_to(queries[None], (PEERS,) + queries.shape)]
    unnamed x12 -> x10, local copies, waits for them, and re-layouts: 1.21 us -> 0.02 us
  transfers between devices with their start and end apart: 3 -> 2, of which waited for: 1 -> 0; matrix products, arithmetic and copies ran while one was open for 1% -> 0% of each run, Pallas kernels for 8% -> 0%
where the time goes in v3:
time: 101 us; the launch traced here: 100 us
  blocking collectives  73.1 us (72%)
  starting transfers between devices  14.9 us (15%)
  Pallas kernels  11.2 us (11%)
    all_gather x1, blocking collectives, local(): kv = lax.all_gather(pair, KEY_AXES, axis=0, tiled=True)  38.3 us
    all_to_all x1, blocking collectives, local(): lax.all_to_all(partial.reshape(8, PIECE, -1), ('yl', 'x'), 0, 0, tiled=True)  19.6 us
    all_to_all x1, blocking collectives, local(): parts = lax.all_to_all(parts, ('z0', 'yh', 'c'), 0, 0, tiled=True)  15.1 us
    ppermute x1, starting transfers between devices, local(): weights = (out_weight, lax.ppermute(late_weight, 'c', [(0, 1), (1, 0)]))  8.55 us
    pallas_call x1, Pallas kernels, attend(): pl.pallas_call(attend_kernel, out_shape=jax.ShapeDtypeStruct((PEERS * 2,...  7.9 us
    all_to_all x1, starting transfers between devices, local(): q = lax.all_to_all(copies, QUERY_AXES, 0, 0, tiled=True)  6.37 us
  transfers between devices with their start and end apart: 2, of which 0 were waited for; matrix products, arithmetic and copies ran while one was open for 0% of the time, Pallas kernels for 0%

profile of v3, /device:TPU:1, one launch (start us, length us, event | category | flops | bytes accessed | tf_op | source)
XLA Modules:
  0.0 100.2 jit_solution(4473829255733765803)
XLA Ops:
  0.0 0.0 copy-start.3
  0.0 0.0 copy-start.4
  0.0 0.0 copy-start.2
  0.0 0.0 copy-start.1
  0.0 1.8 %prepare.1 = (bf16[4,256,256]{2,1,0:T(8,128)(2,1)}, bf16[240,256]{1,0:T(8,128)(2,1)}) custom-call(bf16[256,256]{1,0:T(8,128)(2,1)} %q_ref.1, bf16[240,128]{1,0:T(8,128)(2,1)} %k_ref.1, bf16[240,128]{1,0:T(8,128)(2,1)} %v_ref.1), custom_call_target="tpu_custom_call" | custom-call | tf_op jit(solution)/shard_map/prepare/pallas_call | solution.py:37
  1.9 6.4 %all-to-all-start = ((bf16[4,256,256]{2,1,0:T(8,128)(2,1)}), bf16[4,256,256]{2,1,0:T(8,128)(2,1)}, u32[]{:S(2)}, u32[]{:S(2)}) async-start(bf16[4,256,256]{2,1,0:T(8,128)(2,1)} %get-tuple-element.9), calls=%async_computation | async-start | bytes 1048576 | tf_op jit(solution)/shard_map/all_to_all | solution.py:213
  8.2 0.1 pad_add_fusion.meta
  8.3 38.3 %all_gather.3.kv_ref = bf16[1920,256]{1,0:T(8,128)(2,1)S(1)} all-gather(bf16[240,256]{1,0:T(8,128)(2,1)} %get-tuple-element.10), channel_id=1, replica_groups=mesh['z321'=8,'z0'=2,'yh'=2,'yl'=2,'x'=4,'c'=2] {'z321'}, dimensions={0}, use_global_device_ids=true | all-gather | bytes 1105920 | tf_op jit(solution)/shard_map/document_gather/all_gather | solution.py:215
  46.6 0.0 copy-start
  46.6 0.0 all-to-all-done.q_ref
  46.6 0.0 copy-done.3
  46.6 0.0 copy-done.4
  46.6 0.0 copy-done.2
  46.6 0.0 copy-done.1
  46.7 7.9 %attend.1 = bf16[8,144,256]{2,1,0:T(8,128)(2,1)S(1)} custom-call(s32[4]{0:T(128)S(1)} %pad_add_fusion.meta, f32[16]{0:T(128)S(1)} %copy-done.3, s32[16]{0:T(128)S(1)} %copy-done.4, bf16[4,256,256]{2,1,0:T(8,128)(2,1)} %all-to-all-done.q_ref, bf16[1920,256]{1,0:T(8,128)(2,1)S(1)} %all_gather.3.kv_ref, bf16[256,128]{1,0:T(8,128)(2,1)S(1)} %copy-done.1, ...), custom_call_target="tpu_custom_call" | custom-call | flops 2147483648 | bytes 4194304 | tf_op jit(solution)/shard_map/attend/pallas_call | solution.py:132
  54.6 0.0 copy-done
  54.6 8.6 %collective-permute-start = (bf16[256,4608]{1,0:T(8,128)(2,1)S(1)}, bf16[256,4608]{1,0:T(8,128)(2,1)S(1)}, u32[]{:S(2)}, u32[]{:S(2)}) collective-permute-start(bf16[256,4608]{1,0:T(8,128)(2,1)S(1)} %copy-done), channel_id=1, source_target_pairs={{0,1},{1,0},{2,3},{3,2},{4,5},{5,4},{6,7},{7,6},{8,9},{9,8},{10,11... | collective-permute-start | bytes 7077896 | tf_op jit(solution)/shard_map/ppermute | solution.py:222
  63.1 15.1 %all_to_all.15.parts_ref = bf16[8,144,256]{2,1,0:T(8,128)(2,1)S(1)} all-to-all(bf16[8,144,256]{2,1,0:T(8,128)(2,1)S(1)} %attend.1), channel_id=1, replica_groups=mesh['z321'=8,'z0'=2,'yh'=2,'yl'=2,'x'=4,'c'=2] {'z0','yh','c'}, dimensions={0} | all-to-all | bytes 1179648 | tf_op jit(solution)/shard_map/partials_to_owner/all_to_all | solution.py:221
  78.3 0.0 collective-permute-done.other_ref
  78.3 1.4 %project.1 = bf16[128,4608]{1,0:T(8,128)(2,1)S(1)} custom-call(s32[4]{0:T(128)S(1)} %pad_add_fusion.meta, bf16[8,144,256]{2,1,0:T(8,128)(2,1)S(1)} %all_to_all.15.parts_ref, bf16[256,4608]{1,0:T(8,128)(2,1)S(1)} %copy-done, bf16[256,4608]{1,0:T(8,128)(2,1)S(1)} %collective-permute-done.other_ref), custom_call_target="tpu_custom_call" | custom-call | flops 603979776 | bytes 8388608 | tf_op jit(solution)/shard_map/project/pallas_call | solution.py:185
  79.7 19.6 %all_to_all.16 = bf16[8,16,4608]{2,1,0:T(8,128)(2,1)S(1)} all-to-all(bf16[8,16,4608]{2,1,0:T(8,128)(2,1)S(1)} %bitcast.5), channel_id=1, replica_groups=mesh['z321'=8,'z0'=2,'yh'=2,'yl'=2,'x'=4,'c'=2] {'yl','x'}, dimensions={0} | all-to-all | bytes 2359296 | tf_op jit(solution)/shard_map/heads_exchange/all_to_all | solution.py:225
  99.3 0.9 convert_reduce_fusion
Async XLA Ops:
  0.0 46.6 %copy-start.3 = (f32[16]{0:T(128)S(1)}, f32[16]{0:T(128)}, u32[]{:S(2)}) copy-start(f32[16]{0:T(128)} %caps.1) | copy-start | bytes 196
  0.0 46.6 %copy-start.4 = (s32[16]{0:T(128)S(1)}, s32[16]{0:T(128)}, u32[]{:S(2)}) copy-start(s32[16]{0:T(128)} %lengths.1) | copy-start | bytes 196
  0.0 46.6 %copy-start.2 = (bf16[256,128]{1,0:T(8,128)(2,1)S(1)}, bf16[256,128]{1,0:T(8,128)(2,1)}, u32[]{:S(2)}) copy-start(bf16[256,128]{1,0:T(8,128)(2,1)} %new_v_ref.1) | copy-start | bytes 196612
  0.0 46.6 %copy-start.1 = (bf16[256,128]{1,0:T(8,128)(2,1)S(1)}, bf16[256,128]{1,0:T(8,128)(2,1)}, u32[]{:S(2)}) copy-start(bf16[256,128]{1,0:T(8,128)(2,1)} %new_k_ref.1) | copy-start | bytes 196612
  1.9 44.8 %all-to-all-start = ((bf16[4,256,256]{2,1,0:T(8,128)(2,1)}), bf16[4,256,256]{2,1,0:T(8,128)(2,1)}, u32[]{:S(2)}, u32[]{:S(2)}) async-start(bf16[4,256,256]{2,1,0:T(8,128)(2,1)} %get-tuple-element.9), calls=%async_computation | async-start | bytes 1048576 | tf_op jit(solution)/shard_map/all_to_all | solution.py:213
  46.6 7.9 %copy-start = (bf16[256,4608]{1,0:T(8,128)(2,1)S(1)}, bf16[256,4608]{1,0:T(8,128)(2,1)}, u32[]{:S(2)}) copy-start(bf16[256,4608]{1,0:T(8,128)(2,1)} %mine_ref.1) | copy-start | bytes 7077892
  54.6 23.7 %collective-permute-start = (bf16[256,4608]{1,0:T(8,128)(2,1)S(1)}, bf16[256,4608]{1,0:T(8,128)(2,1)S(1)}, u32[]{:S(2)}, u32[]{:S(2)}) collective-permute-start(bf16[256,4608]{1,0:T(8,128)(2,1)S(1)} %copy-done), channel_id=1, source_target_pairs={{0,1},{1,0},{2,3},{3,2},{4,5},{5,4},{6,7},{7,6},{8,9},{9,8},{10,11... | collective-permute-start | bytes 7077896 | tf_op jit(solution)/shard_map/ppermute | solution.py:222

commit v4 on v3

--- a/solution.py
+++ b/solution.py
@@ -47,8 +47,10 @@
 
 
 def attend_kernel(
-    meta, caps, lengths, q_ref, kv_ref, new_k_ref, new_v_ref, out_ref, acc_ref
+    meta, caps, lengths, q_ref, kv_ref, new_k_ref, new_v_ref, out_ref, acc_ref, totals_ref
 ):
+    totals_ref[...] = jnp.zeros_like(totals_ref)
+
     def serve(peer):
         tokens = q_ref.shape[1]
         new_keys = new_k_ref.shape[0]
@@ -107,20 +109,28 @@
                     out_ref[2 * peer + c, j * PIECE : (j + 1) * PIECE, cols] = acc_ref[
                         rows[j] : rows[j] + PIECE, :HD
                     ].astype(out_ref.dtype)
-                totals = jnp.concatenate(
-                    [acc_ref[r : r + PIECE, HD:] for r in rows], axis=0
-                ).T[:META]
-                high = totals.astype(jnp.bfloat16).astype(jnp.float32)
-                index = lax.broadcasted_iota(jnp.int32, totals.shape, 0)
-                out_ref[2 * peer + c, tokens // 2 :, cols] = jnp.where(
-                    index == 0, high, totals - high
-                ).astype(out_ref.dtype)
+                totals = jnp.concatenate([acc_ref[r : r + PIECE, HD:] for r in rows], axis=0)
+                lane = lax.broadcasted_iota(jnp.int32, totals.shape, 1)
+                place = (2 * peer + c) * GROUP + head
+                totals_ref[...] = jnp.where(lane == place, totals, totals_ref[...])
 
     def step(peer, carry):
         serve(peer)
         return carry
 
     lax.fori_loop(0, PEERS, step, 0)
+
+    low_rows = totals_ref[...].T[: 2 * PEERS * GROUP]
+    high_rows = low_rows.astype(jnp.bfloat16).astype(jnp.float32)
+    low_rows = low_rows - high_rows
+    first = lax.broadcasted_iota(jnp.int32, (META, HD), 0) == 0
+    for target in range(2 * PEERS):
+        for head in range(GROUP):
+            row = slice(target * GROUP + head, target * GROUP + head + 1)
+            pair = jnp.where(first, high_rows[row], low_rows[row])
+            out_ref[target, out_ref.shape[1] - META :, head * HD : (head + 1) * HD] = pair.astype(
+                out_ref.dtype
+            )
 
 
 def attend(meta, caps, lengths, q, kv, new_k, new_v):
@@ -136,7 +146,10 @@
         ),
         in_specs=[smem, smem, smem, vmem, vmem, vmem, vmem],
         out_specs=vmem,
-        scratch_shapes=[pltpu.VMEM((GROUP * tokens, 2 * HD), jnp.float32)],
+        scratch_shapes=[
+            pltpu.VMEM((GROUP * tokens, 2 * HD), jnp.float32),
+            pltpu.VMEM((tokens // 2, HD), jnp.float32),
+        ],
         compiler_params=pltpu.CompilerParams(
             vmem_limit_bytes=40 * 1024 * 1024,
         ),

time: 101 us -> 101 us (level)
  no operation moved by 1% of the time
where the time goes in v4:
time: 101 us; the launch traced here: 100 us
  blocking collectives  73.4 us (73%)
  starting transfers between devices  14.9 us (15%)
  Pallas kernels  10.9 us (11%)
    all_gather x1, blocking collectives, local(): kv = lax.all_gather(pair, KEY_AXES, axis=0, tiled=True)  38.3 us
    all_to_all x1, blocking collectives, local(): lax.all_to_all(partial.reshape(8, PIECE, -1), ('yl', 'x'), 0, 0, tiled=True)  20 us
    all_to_all x1, blocking collectives, local(): parts = lax.all_to_all(parts, ('z0', 'yh', 'c'), 0, 0, tiled=True)  15.1 us
    ppermute x1, starting transfers between devices, local(): weights = (out_weight, lax.ppermute(late_weight, 'c', [(0, 1), (1, 0)]))  8.55 us
    pallas_call x1, Pallas kernels, attend(): pl.pallas_call(attend_kernel, out_shape=jax.ShapeDtypeStruct((PEERS * 2,...  7.69 us
    all_to_all x1, starting transfers between devices, local(): q = lax.all_to_all(copies, QUERY_AXES, 0, 0, tiled=True)  6.37 us
  transfers between devices with their start and end apart: 2, of which 0 were waited for; matrix products, arithmetic and copies ran while one was open for 0% of the time, Pallas kernels for 0%

profile of v4, /device:TPU:1, one launch (start us, length us, event | category | flops | bytes accessed | tf_op | source)
XLA Modules:
  0.0 100.3 jit_solution(10061757189235326255)
XLA Ops:
  0.0 0.0 copy-start.3
  0.0 0.0 copy-start.4
  0.0 0.0 copy-start.2
  0.0 0.0 copy-start.1
  0.0 1.8 %prepare.1 = (bf16[4,256,256]{2,1,0:T(8,128)(2,1)}, bf16[240,256]{1,0:T(8,128)(2,1)}) custom-call(bf16[256,256]{1,0:T(8,128)(2,1)} %q_ref.1, bf16[240,128]{1,0:T(8,128)(2,1)} %k_ref.1, bf16[240,128]{1,0:T(8,128)(2,1)} %v_ref.1), custom_call_target="tpu_custom_call" | custom-call | tf_op jit(solution)/shard_map/prepare/pallas_call | solution.py:37
  1.9 6.4 %all-to-all-start = ((bf16[4,256,256]{2,1,0:T(8,128)(2,1)}), bf16[4,256,256]{2,1,0:T(8,128)(2,1)}, u32[]{:S(2)}, u32[]{:S(2)}) async-start(bf16[4,256,256]{2,1,0:T(8,128)(2,1)} %get-tuple-element.9), calls=%async_computation | async-start | bytes 1048576 | tf_op jit(solution)/shard_map/all_to_all | solution.py:226
  8.2 0.1 pad_add_fusion.meta
  8.3 38.3 %all_gather.3.kv_ref = bf16[1920,256]{1,0:T(8,128)(2,1)S(1)} all-gather(bf16[240,256]{1,0:T(8,128)(2,1)} %get-tuple-element.10), channel_id=1, replica_groups=mesh['z321'=8,'z0'=2,'yh'=2,'yl'=2,'x'=4,'c'=2] {'z321'}, dimensions={0}, use_global_device_ids=true | all-gather | bytes 1105920 | tf_op jit(solution)/shard_map/document_gather/all_gather | solution.py:228
  46.6 0.0 copy-start
  46.6 0.0 all-to-all-done.q_ref
  46.6 0.0 copy-done.3
  46.6 0.0 copy-done.4
  46.6 0.0 copy-done.2
  46.6 0.0 copy-done.1
  46.7 7.7 %attend.1 = bf16[8,144,256]{2,1,0:T(8,128)(2,1)S(1)} custom-call(s32[4]{0:T(128)S(1)} %pad_add_fusion.meta, f32[16]{0:T(128)S(1)} %copy-done.3, s32[16]{0:T(128)S(1)} %copy-done.4, bf16[4,256,256]{2,1,0:T(8,128)(2,1)} %all-to-all-done.q_ref, bf16[1920,256]{1,0:T(8,128)(2,1)S(1)} %all_gather.3.kv_ref, bf16[256,128]{1,0:T(8,128)(2,1)S(1)} %copy-done.1, ...), custom_call_target="tpu_custom_call" | custom-call | flops 2147483648 | bytes 4194304 | tf_op jit(solution)/shard_map/attend/pallas_call | solution.py:142
  54.4 0.0 copy-done
  54.4 8.6 %collective-permute-start = (bf16[256,4608]{1,0:T(8,128)(2,1)S(1)}, bf16[256,4608]{1,0:T(8,128)(2,1)S(1)}, u32[]{:S(2)}, u32[]{:S(2)}) collective-permute-start(bf16[256,4608]{1,0:T(8,128)(2,1)S(1)} %copy-done), channel_id=1, source_target_pairs={{0,1},{1,0},{2,3},{3,2},{4,5},{5,4},{6,7},{7,6},{8,9},{9,8},{10,11... | collective-permute-start | bytes 7077896 | tf_op jit(solution)/shard_map/ppermute | solution.py:235
  62.9 15.1 %all_to_all.15.parts_ref = bf16[8,144,256]{2,1,0:T(8,128)(2,1)S(1)} all-to-all(bf16[8,144,256]{2,1,0:T(8,128)(2,1)S(1)} %attend.1), channel_id=1, replica_groups=mesh['z321'=8,'z0'=2,'yh'=2,'yl'=2,'x'=4,'c'=2] {'z0','yh','c'}, dimensions={0} | all-to-all | bytes 1179648 | tf_op jit(solution)/shard_map/partials_to_owner/all_to_all | solution.py:234
  78.1 0.0 collective-permute-done.other_ref
  78.1 1.4 %project.1 = bf16[128,4608]{1,0:T(8,128)(2,1)S(1)} custom-call(s32[4]{0:T(128)S(1)} %pad_add_fusion.meta, bf16[8,144,256]{2,1,0:T(8,128)(2,1)S(1)} %all_to_all.15.parts_ref, bf16[256,4608]{1,0:T(8,128)(2,1)S(1)} %copy-done, bf16[256,4608]{1,0:T(8,128)(2,1)S(1)} %collective-permute-done.other_ref), custom_call_target="tpu_custom_call" | custom-call | flops 603979776 | bytes 8388608 | tf_op jit(solution)/shard_map/project/pallas_call | solution.py:198
  79.5 20.0 %all_to_all.16 = bf16[8,16,4608]{2,1,0:T(8,128)(2,1)S(1)} all-to-all(bf16[8,16,4608]{2,1,0:T(8,128)(2,1)S(1)} %bitcast.5), channel_id=1, replica_groups=mesh['z321'=8,'z0'=2,'yh'=2,'yl'=2,'x'=4,'c'=2] {'yl','x'}, dimensions={0} | all-to-all | bytes 2359296 | tf_op jit(solution)/shard_map/heads_exchange/all_to_all | solution.py:238
  99.4 0.9 convert_reduce_fusion
Async XLA Ops:
  0.0 46.6 %copy-start.3 = (f32[16]{0:T(128)S(1)}, f32[16]{0:T(128)}, u32[]{:S(2)}) copy-start(f32[16]{0:T(128)} %caps.1) | copy-start | bytes 196
  0.0 46.6 %copy-start.4 = (s32[16]{0:T(128)S(1)}, s32[16]{0:T(128)}, u32[]{:S(2)}) copy-start(s32[16]{0:T(128)} %lengths.1) | copy-start | bytes 196
  0.0 46.6 %copy-start.2 = (bf16[256,128]{1,0:T(8,128)(2,1)S(1)}, bf16[256,128]{1,0:T(8,128)(2,1)}, u32[]{:S(2)}) copy-start(bf16[256,128]{1,0:T(8,128)(2,1)} %new_v_ref.1) | copy-start | bytes 196612
  0.0 46.6 %copy-start.1 = (bf16[256,128]{1,0:T(8,128)(2,1)S(1)}, bf16[256,128]{1,0:T(8,128)(2,1)}, u32[]{:S(2)}) copy-start(bf16[256,128]{1,0:T(8,128)(2,1)} %new_k_ref.1) | copy-start | bytes 196612
  1.9 44.8 %all-to-all-start = ((bf16[4,256,256]{2,1,0:T(8,128)(2,1)}), bf16[4,256,256]{2,1,0:T(8,128)(2,1)}, u32[]{:S(2)}, u32[]{:S(2)}) async-start(bf16[4,256,256]{2,1,0:T(8,128)(2,1)} %get-tuple-element.9), calls=%async_computation | async-start | bytes 1048576 | tf_op jit(solution)/shard_map/all_to_all | solution.py:226
  46.6 7.7 %copy-start = (bf16[256,4608]{1,0:T(8,128)(2,1)S(1)}, bf16[256,4608]{1,0:T(8,128)(2,1)}, u32[]{:S(2)}) copy-start(bf16[256,4608]{1,0:T(8,128)(2,1)} %mine_ref.1) | copy-start | bytes 7077892
  54.4 23.7 %collective-permute-start = (bf16[256,4608]{1,0:T(8,128)(2,1)S(1)}, bf16[256,4608]{1,0:T(8,128)(2,1)S(1)}, u32[]{:S(2)}, u32[]{:S(2)}) collective-permute-start(bf16[256,4608]{1,0:T(8,128)(2,1)S(1)} %copy-done), channel_id=1, source_target_pairs={{0,1},{1,0},{2,3},{3,2},{4,5},{5,4},{6,7},{7,6},{8,9},{9,8},{10,11... | collective-permute-start | bytes 7077896 | tf_op jit(solution)/shard_map/ppermute | solution.py:235

commit v5 on v4

--- a/solution.py
+++ b/solution.py
@@ -56,7 +56,7 @@
         new_keys = new_k_ref.shape[0]
         z_base, my_z0, my_yh = meta[0], meta[1], meta[2]
         peer_z0 = peer // 2
-        peer_yh = lax.rem(peer, 2)
+        peer_yh = peer % 2
         request = z_base + peer_z0
         cap = jnp.full((1, 1), caps[request], jnp.float32)
         inner = SCALE / cap
@@ -114,11 +114,8 @@
                 place = (2 * peer + c) * GROUP + head
                 totals_ref[...] = jnp.where(lane == place, totals, totals_ref[...])
 
-    def step(peer, carry):
+    for peer in range(PEERS):
         serve(peer)
-        return carry
-
-    lax.fori_loop(0, PEERS, step, 0)
 
     low_rows = totals_ref[...].T[: 2 * PEERS * GROUP]
     high_rows = low_rows.astype(jnp.bfloat16).astype(jnp.float32)

time: 101 us -> 101 us (level)
  no operation moved by 1% of the time
where the time goes in v5:
time: 101 us; the launch traced here: 100 us
  blocking collectives  73.4 us (73%)
  starting transfers between devices  14.9 us (15%)
  Pallas kernels  10.9 us (11%)
    all_gather x1, blocking collectives, local(): kv = lax.all_gather(pair, KEY_AXES, axis=0, tiled=True)  38.3 us
    all_to_all x1, blocking collectives, local(): lax.all_to_all(partial.reshape(8, PIECE, -1), ('yl', 'x'), 0, 0, tiled=True)  20 us
    all_to_all x1, blocking collectives, local(): parts = lax.all_to_all(parts, ('z0', 'yh', 'c'), 0, 0, tiled=True)  15.1 us
    ppermute x1, starting transfers between devices, local(): weights = (out_weight, lax.ppermute(late_weight, 'c', [(0, 1), (1, 0)]))  8.56 us
    pallas_call x1, Pallas kernels, attend(): pl.pallas_call(attend_kernel, out_shape=jax.ShapeDtypeStruct((PEERS * 2,...  7.65 us
    all_to_all x1, starting transfers between devices, local(): q = lax.all_to_all(copies, QUERY_AXES, 0, 0, tiled=True)  6.37 us
  transfers between devices with their start and end apart: 2, of which 0 were waited for; matrix products, arithmetic and copies ran while one was open for 0% of the time, Pallas kernels for 0%

profile of v5, /device:TPU:1, one launch (start us, length us, event | category | flops | bytes accessed | tf_op | source)
XLA Modules:
  0.0 100.3 jit_solution(17101977331929549417)
XLA Ops:
  0.0 0.0 copy-start.3
  0.0 0.0 copy-start.4
  0.0 0.0 copy-start.2
  0.0 0.0 copy-start.1
  0.0 1.8 %prepare.1 = (bf16[4,256,256]{2,1,0:T(8,128)(2,1)}, bf16[240,256]{1,0:T(8,128)(2,1)}) custom-call(bf16[256,256]{1,0:T(8,128)(2,1)} %q_ref.1, bf16[240,128]{1,0:T(8,128)(2,1)} %k_ref.1, bf16[240,128]{1,0:T(8,128)(2,1)} %v_ref.1), custom_call_target="tpu_custom_call" | custom-call | tf_op jit(solution)/shard_map/prepare/pallas_call | solution.py:37
  1.9 6.4 %all-to-all-start = ((bf16[4,256,256]{2,1,0:T(8,128)(2,1)}), bf16[4,256,256]{2,1,0:T(8,128)(2,1)}, u32[]{:S(2)}, u32[]{:S(2)}) async-start(bf16[4,256,256]{2,1,0:T(8,128)(2,1)} %get-tuple-element.9), calls=%async_computation | async-start | bytes 1048576 | tf_op jit(solution)/shard_map/all_to_all | solution.py:223
  8.2 0.1 pad_add_fusion.meta
  8.3 38.3 %all_gather.3.kv_ref = bf16[1920,256]{1,0:T(8,128)(2,1)S(1)} all-gather(bf16[240,256]{1,0:T(8,128)(2,1)} %get-tuple-element.10), channel_id=1, replica_groups=mesh['z321'=8,'z0'=2,'yh'=2,'yl'=2,'x'=4,'c'=2] {'z321'}, dimensions={0}, use_global_device_ids=true | all-gather | bytes 1105920 | tf_op jit(solution)/shard_map/document_gather/all_gather | solution.py:225
  46.6 0.0 copy-start
  46.6 0.0 all-to-all-done.q_ref
  46.6 0.0 copy-done.3
  46.6 0.0 copy-done.4
  46.6 0.0 copy-done.2
  46.6 0.0 copy-done.1
  46.7 7.7 %attend.1 = bf16[8,144,256]{2,1,0:T(8,128)(2,1)S(1)} custom-call(s32[4]{0:T(128)S(1)} %pad_add_fusion.meta, f32[16]{0:T(128)S(1)} %copy-done.3, s32[16]{0:T(128)S(1)} %copy-done.4, bf16[4,256,256]{2,1,0:T(8,128)(2,1)} %all-to-all-done.q_ref, bf16[1920,256]{1,0:T(8,128)(2,1)S(1)} %all_gather.3.kv_ref, bf16[256,128]{1,0:T(8,128)(2,1)S(1)} %copy-done.1, ...), custom_call_target="tpu_custom_call" | custom-call | flops 2147483648 | bytes 4194304 | tf_op jit(solution)/shard_map/attend/pallas_call | solution.py:139
  54.3 0.0 copy-done
  54.3 8.6 %collective-permute-start = (bf16[256,4608]{1,0:T(8,128)(2,1)S(1)}, bf16[256,4608]{1,0:T(8,128)(2,1)S(1)}, u32[]{:S(2)}, u32[]{:S(2)}) collective-permute-start(bf16[256,4608]{1,0:T(8,128)(2,1)S(1)} %copy-done), channel_id=1, source_target_pairs={{0,1},{1,0},{2,3},{3,2},{4,5},{5,4},{6,7},{7,6},{8,9},{9,8},{10,11... | collective-permute-start | bytes 7077896 | tf_op jit(solution)/shard_map/ppermute | solution.py:232
  62.9 15.1 %all_to_all.15.parts_ref = bf16[8,144,256]{2,1,0:T(8,128)(2,1)S(1)} all-to-all(bf16[8,144,256]{2,1,0:T(8,128)(2,1)S(1)} %attend.1), channel_id=1, replica_groups=mesh['z321'=8,'z0'=2,'yh'=2,'yl'=2,'x'=4,'c'=2] {'z0','yh','c'}, dimensions={0} | all-to-all | bytes 1179648 | tf_op jit(solution)/shard_map/partials_to_owner/all_to_all | solution.py:231
  78.0 0.0 collective-permute-done.other_ref
  78.0 1.4 %project.1 = bf16[128,4608]{1,0:T(8,128)(2,1)S(1)} custom-call(s32[4]{0:T(128)S(1)} %pad_add_fusion.meta, bf16[8,144,256]{2,1,0:T(8,128)(2,1)S(1)} %all_to_all.15.parts_ref, bf16[256,4608]{1,0:T(8,128)(2,1)S(1)} %copy-done, bf16[256,4608]{1,0:T(8,128)(2,1)S(1)} %collective-permute-done.other_ref), custom_call_target="tpu_custom_call" | custom-call | flops 603979776 | bytes 8388608 | tf_op jit(solution)/shard_map/project/pallas_call | solution.py:195
  79.5 20.0 %all_to_all.16 = bf16[8,16,4608]{2,1,0:T(8,128)(2,1)S(1)} all-to-all(bf16[8,16,4608]{2,1,0:T(8,128)(2,1)S(1)} %bitcast.5), channel_id=1, replica_groups=mesh['z321'=8,'z0'=2,'yh'=2,'yl'=2,'x'=4,'c'=2] {'yl','x'}, dimensions={0} | all-to-all | bytes 2359296 | tf_op jit(solution)/shard_map/heads_exchange/all_to_all | solution.py:235
  99.4 0.9 convert_reduce_fusion
Async XLA Ops:
  0.0 46.6 %copy-start.3 = (f32[16]{0:T(128)S(1)}, f32[16]{0:T(128)}, u32[]{:S(2)}) copy-start(f32[16]{0:T(128)} %caps.1) | copy-start | bytes 196
  0.0 46.6 %copy-start.4 = (s32[16]{0:T(128)S(1)}, s32[16]{0:T(128)}, u32[]{:S(2)}) copy-start(s32[16]{0:T(128)} %lengths.1) | copy-start | bytes 196
  0.0 46.6 %copy-start.2 = (bf16[256,128]{1,0:T(8,128)(2,1)S(1)}, bf16[256,128]{1,0:T(8,128)(2,1)}, u32[]{:S(2)}) copy-start(bf16[256,128]{1,0:T(8,128)(2,1)} %new_v_ref.1) | copy-start | bytes 196612
  0.0 46.6 %copy-start.1 = (bf16[256,128]{1,0:T(8,128)(2,1)S(1)}, bf16[256,128]{1,0:T(8,128)(2,1)}, u32[]{:S(2)}) copy-start(bf16[256,128]{1,0:T(8,128)(2,1)} %new_k_ref.1) | copy-start | bytes 196612
  1.9 44.8 %all-to-all-start = ((bf16[4,256,256]{2,1,0:T(8,128)(2,1)}), bf16[4,256,256]{2,1,0:T(8,128)(2,1)}, u32[]{:S(2)}, u32[]{:S(2)}) async-start(bf16[4,256,256]{2,1,0:T(8,128)(2,1)} %get-tuple-element.9), calls=%async_computation | async-start | bytes 1048576 | tf_op jit(solution)/shard_map/all_to_all | solution.py:223
  46.6 7.7 %copy-start = (bf16[256,4608]{1,0:T(8,128)(2,1)S(1)}, bf16[256,4608]{1,0:T(8,128)(2,1)}, u32[]{:S(2)}) copy-start(bf16[256,4608]{1,0:T(8,128)(2,1)} %mine_ref.1) | copy-start | bytes 7077892
  54.3 23.7 %collective-permute-start = (bf16[256,4608]{1,0:T(8,128)(2,1)S(1)}, bf16[256,4608]{1,0:T(8,128)(2,1)S(1)}, u32[]{:S(2)}, u32[]{:S(2)}) collective-permute-start(bf16[256,4608]{1,0:T(8,128)(2,1)S(1)} %copy-done), channel_id=1, source_target_pairs={{0,1},{1,0},{2,3},{3,2},{4,5},{5,4},{6,7},{7,6},{8,9},{9,8},{10,11... | collective-permute-start | bytes 7077896 | tf_op jit(solution)/shard_map/ppermute | solution.py:232

commit v6 on v5

--- a/solution.py
+++ b/solution.py
@@ -22,7 +22,7 @@
 PEERS = 4
 PIECE = 16
 META = 16
-BLOCK = 768
+BLOCK = 1536
 
 
 def prepare_kernel(q_ref, k_ref, v_ref, copies_ref, kv_ref):

time: 101 us -> 101 us (level)
  no operation moved by 1% of the time
where the time goes in v6:
time: 101 us; the launch traced here: 100 us
  blocking collectives  73.4 us (73%)
  starting transfers between devices  14.9 us (15%)
  Pallas kernels  10.9 us (11%)
    all_gather x1, blocking collectives, local(): kv = lax.all_gather(pair, KEY_AXES, axis=0, tiled=True)  38.3 us
    all_to_all x1, blocking collectives, local(): lax.all_to_all(partial.reshape(8, PIECE, -1), ('yl', 'x'), 0, 0, tiled=True)  19.9 us
    all_to_all x1, blocking collectives, local(): parts = lax.all_to_all(parts, ('z0', 'yh', 'c'), 0, 0, tiled=True)  15.1 us
    ppermute x1, starting transfers between devices, local(): weights = (out_weight, lax.ppermute(late_weight, 'c', [(0, 1), (1, 0)]))  8.56 us
    pallas_call x1, Pallas kernels, attend(): pl.pallas_call(attend_kernel, out_shape=jax.ShapeDtypeStruct((PEERS * 2,...  7.65 us
    all_to_all x1, starting transfers between devices, local(): q = lax.all_to_all(copies, QUERY_AXES, 0, 0, tiled=True)  6.37 us
  transfers between devices with their start and end apart: 2, of which 0 were waited for; matrix products, arithmetic and copies ran while one was open for 0% of the time, Pallas kernels for 0%

profile of v6, /device:TPU:1, one launch (start us, length us, event | category | flops | bytes accessed | tf_op | source)
XLA Modules:
  0.0 100.2 jit_solution(11200413530436420240)
XLA Ops:
  0.0 0.0 copy-start.3
  0.0 0.0 copy-start.4
  0.0 0.0 copy-start.2
  0.0 0.0 copy-start.1
  0.0 1.8 %prepare.1 = (bf16[4,256,256]{2,1,0:T(8,128)(2,1)}, bf16[240,256]{1,0:T(8,128)(2,1)}) custom-call(bf16[256,256]{1,0:T(8,128)(2,1)} %q_ref.1, bf16[240,128]{1,0:T(8,128)(2,1)} %k_ref.1, bf16[240,128]{1,0:T(8,128)(2,1)} %v_ref.1), custom_call_target="tpu_custom_call" | custom-call | tf_op jit(solution)/shard_map/prepare/pallas_call | solution.py:37
  1.9 6.4 %all-to-all-start = ((bf16[4,256,256]{2,1,0:T(8,128)(2,1)}), bf16[4,256,256]{2,1,0:T(8,128)(2,1)}, u32[]{:S(2)}, u32[]{:S(2)}) async-start(bf16[4,256,256]{2,1,0:T(8,128)(2,1)} %get-tuple-element.9), calls=%async_computation | async-start | bytes 1048576 | tf_op jit(solution)/shard_map/all_to_all | solution.py:223
  8.2 0.1 pad_add_fusion.meta
  8.3 38.3 %all_gather.3.kv_ref = bf16[1920,256]{1,0:T(8,128)(2,1)S(1)} all-gather(bf16[240,256]{1,0:T(8,128)(2,1)} %get-tuple-element.10), channel_id=1, replica_groups=mesh['z321'=8,'z0'=2,'yh'=2,'yl'=2,'x'=4,'c'=2] {'z321'}, dimensions={0}, use_global_device_ids=true | all-gather | bytes 1105920 | tf_op jit(solution)/shard_map/document_gather/all_gather | solution.py:225
  46.6 0.0 copy-start
  46.6 0.0 all-to-all-done.q_ref
  46.6 0.0 copy-done.3
  46.6 0.0 copy-done.4
  46.6 0.0 copy-done.2
  46.6 0.0 copy-done.1
  46.7 7.7 %attend.1 = bf16[8,144,256]{2,1,0:T(8,128)(2,1)S(1)} custom-call(s32[4]{0:T(128)S(1)} %pad_add_fusion.meta, f32[16]{0:T(128)S(1)} %copy-done.3, s32[16]{0:T(128)S(1)} %copy-done.4, bf16[4,256,256]{2,1,0:T(8,128)(2,1)} %all-to-all-done.q_ref, bf16[1920,256]{1,0:T(8,128)(2,1)S(1)} %all_gather.3.kv_ref, bf16[256,128]{1,0:T(8,128)(2,1)S(1)} %copy-done.1, ...), custom_call_target="tpu_custom_call" | custom-call | flops 2147483648 | bytes 4194304 | tf_op jit(solution)/shard_map/attend/pallas_call | solution.py:139
  54.3 0.0 copy-done
  54.3 8.6 %collective-permute-start = (bf16[256,4608]{1,0:T(8,128)(2,1)S(1)}, bf16[256,4608]{1,0:T(8,128)(2,1)S(1)}, u32[]{:S(2)}, u32[]{:S(2)}) collective-permute-start(bf16[256,4608]{1,0:T(8,128)(2,1)S(1)} %copy-done), channel_id=1, source_target_pairs={{0,1},{1,0},{2,3},{3,2},{4,5},{5,4},{6,7},{7,6},{8,9},{9,8},{10,11... | collective-permute-start | bytes 7077896 | tf_op jit(solution)/shard_map/ppermute | solution.py:232
  62.9 15.1 %all_to_all.15.parts_ref = bf16[8,144,256]{2,1,0:T(8,128)(2,1)S(1)} all-to-all(bf16[8,144,256]{2,1,0:T(8,128)(2,1)S(1)} %attend.1), channel_id=1, replica_groups=mesh['z321'=8,'z0'=2,'yh'=2,'yl'=2,'x'=4,'c'=2] {'z0','yh','c'}, dimensions={0} | all-to-all | bytes 1179648 | tf_op jit(solution)/shard_map/partials_to_owner/all_to_all | solution.py:231
  78.0 0.0 collective-permute-done.other_ref
  78.0 1.4 %project.1 = bf16[128,4608]{1,0:T(8,128)(2,1)S(1)} custom-call(s32[4]{0:T(128)S(1)} %pad_add_fusion.meta, bf16[8,144,256]{2,1,0:T(8,128)(2,1)S(1)} %all_to_all.15.parts_ref, bf16[256,4608]{1,0:T(8,128)(2,1)S(1)} %copy-done, bf16[256,4608]{1,0:T(8,128)(2,1)S(1)} %collective-permute-done.other_ref), custom_call_target="tpu_custom_call" | custom-call | flops 603979776 | bytes 8388608 | tf_op jit(solution)/shard_map/project/pallas_call | solution.py:195
  79.4 19.9 %all_to_all.16 = bf16[8,16,4608]{2,1,0:T(8,128)(2,1)S(1)} all-to-all(bf16[8,16,4608]{2,1,0:T(8,128)(2,1)S(1)} %bitcast.5), channel_id=1, replica_groups=mesh['z321'=8,'z0'=2,'yh'=2,'yl'=2,'x'=4,'c'=2] {'yl','x'}, dimensions={0} | all-to-all | bytes 2359296 | tf_op jit(solution)/shard_map/heads_exchange/all_to_all | solution.py:235
  99.4 0.9 convert_reduce_fusion
Async XLA Ops:
  0.0 46.6 %copy-start.3 = (f32[16]{0:T(128)S(1)}, f32[16]{0:T(128)}, u32[]{:S(2)}) copy-start(f32[16]{0:T(128)} %caps.1) | copy-start | bytes 196
  0.0 46.6 %copy-start.4 = (s32[16]{0:T(128)S(1)}, s32[16]{0:T(128)}, u32[]{:S(2)}) copy-start(s32[16]{0:T(128)} %lengths.1) | copy-start | bytes 196
  0.0 46.6 %copy-start.2 = (bf16[256,128]{1,0:T(8,128)(2,1)S(1)}, bf16[256,128]{1,0:T(8,128)(2,1)}, u32[]{:S(2)}) copy-start(bf16[256,128]{1,0:T(8,128)(2,1)} %new_v_ref.1) | copy-start | bytes 196612
  0.0 46.6 %copy-start.1 = (bf16[256,128]{1,0:T(8,128)(2,1)S(1)}, bf16[256,128]{1,0:T(8,128)(2,1)}, u32[]{:S(2)}) copy-start(bf16[256,128]{1,0:T(8,128)(2,1)} %new_k_ref.1) | copy-start | bytes 196612
  1.9 44.8 %all-to-all-start = ((bf16[4,256,256]{2,1,0:T(8,128)(2,1)}), bf16[4,256,256]{2,1,0:T(8,128)(2,1)}, u32[]{:S(2)}, u32[]{:S(2)}) async-start(bf16[4,256,256]{2,1,0:T(8,128)(2,1)} %get-tuple-element.9), calls=%async_computation | async-start | bytes 1048576 | tf_op jit(solution)/shard_map/all_to_all | solution.py:223
  46.6 7.7 %copy-start = (bf16[256,4608]{1,0:T(8,128)(2,1)S(1)}, bf16[256,4608]{1,0:T(8,128)(2,1)}, u32[]{:S(2)}) copy-start(bf16[256,4608]{1,0:T(8,128)(2,1)} %mine_ref.1) | copy-start | bytes 7077892
  54.3 23.7 %collective-permute-start = (bf16[256,4608]{1,0:T(8,128)(2,1)S(1)}, bf16[256,4608]{1,0:T(8,128)(2,1)S(1)}, u32[]{:S(2)}, u32[]{:S(2)}) collective-permute-start(bf16[256,4608]{1,0:T(8,128)(2,1)S(1)} %copy-done), channel_id=1, source_target_pairs={{0,1},{1,0},{2,3},{3,2},{4,5},{5,4},{6,7},{7,6},{8,9},{9,8},{10,11... | collective-permute-start | bytes 7077896 | tf_op jit(solution)/shard_map/ppermute | solution.py:232
